TPU v7x, 32 devices: a whole 2x2x4 slice. The times are simulated.
32 devices in a mesh: batch: 2 (over y), seq: 16 (over z, x, core).
Axes of the slice: x: 2, y: 2, z: 4, core: 2. Of those that a mesh axis runs over, the one named last changes fastest.
Arguments:
- inputs: bfloat16 [2, 4, 2048, 768], P(None, 'batch', 'seq'), may hold values from -6 to 6
- seg_ids: int32 [2, 4, 2048], P(None, 'batch', 'seq'), may hold values from 0 to 8, as said below
- cotangent: bfloat16 [2, 4, 2048, 768], P(None, 'batch', 'seq'), may hold values from -6 to 6
- projection: bfloat16 [12, 64, 256], replicated, may hold values from -6 to 6
- w_qkv: bfloat16 [768, 2304], P(('batch', 'seq')), may hold values from -0.21875 to 0.21875
- b_qkv: bfloat16 [2304], P(('batch', 'seq')), may hold values from -4 to 4
- w_o: bfloat16 [768, 768], P(('batch', 'seq')), may hold values from -1.25 to 1.25
- b_o: bfloat16 [768], P(('batch', 'seq')), may hold values from -4 to 4
- ln1_gain: bfloat16 [768], P(('batch', 'seq')), may hold values from 0.099609375 to 1.8984375
- ln1_bias: bfloat16 [768], P(('batch', 'seq')), may hold values from -4 to 4
- w_in: bfloat16 [768, 3072], P(('batch', 'seq')), may hold values from -0.21875 to 0.21875
- b_in: bfloat16 [3072], P(('batch', 'seq')), may hold values from -4 to 4
- w_out: bfloat16 [3072, 768], P(('batch', 'seq')), may hold values from -0.109375 to 0.109375
- b_out: bfloat16 [768], P(('batch', 'seq')), may hold values from -4 to 4
- ln2_gain: bfloat16 [768], P(('batch', 'seq')), may hold values from 0.099609375 to 1.8984375
- ln2_bias: bfloat16 [768], P(('batch', 'seq')), may hold values from -4 to 4
Outputs:
- output: bfloat16 [2, 4, 2048, 768], P(None, 'batch', 'seq')
- input_grad: bfloat16 [2, 4, 2048, 768], P(None, 'batch', 'seq')
- grad_w_qkv: float32 [768, 2304], P(('batch', 'seq'))
- grad_b_qkv: float32 [2304], P(('batch', 'seq'))
- grad_w_o: float32 [768, 768], P(('batch', 'seq'))
- grad_b_o: float32 [768], P(('batch', 'seq'))
- grad_ln1_gain: float32 [768], P(('batch', 'seq'))
- grad_ln1_bias: float32 [768], P(('batch', 'seq'))
- grad_w_in: float32 [768, 3072], P(('batch', 'seq'))
- grad_b_in: float32 [3072], P(('batch', 'seq'))
- grad_w_out: float32 [3072, 768], P(('batch', 'seq'))
- grad_b_out: float32 [768], P(('batch', 'seq'))
- grad_ln2_gain: float32 [768], P(('batch', 'seq'))
- grad_ln2_bias: float32 [768], P(('batch', 'seq'))
Inputs may be any that keep to these rules, and one draw needn't show every extreme that they name: `seg_ids`: along each sequence the ids start at 0 and rise by 0 or 1 from one token to the next; equal ids form one segment. Of the 2 sequences that share a micro-batch and an index of batch, one is a single segment; each of the others has exactly 16 // 2 + 1 segments.
All inputs are finite; a program needn't handle non-finite values.
Results may differ from a plain program's by a relative error of at most 0.03.
Values may be sent and summed in bfloat16 or wider, within the bound.
No kernel may reach another device: no remote copies, remote signals or barrier semaphores. Data moves between devices by JAX's collectives and lax.ppermute only.
A program may use at most 320 MiB of HBM per device.

v0:
```python
import math
from functools import partial

import jax
import jax.numpy as jnp
from jax import lax
from jax.experimental import pallas as pl
from jax.experimental.pallas import tpu as pltpu
from jax.sharding import PartitionSpec as P

norm_eps = 1e-05
bf16 = jnp.bfloat16
f32 = jnp.float32
AXES = ("batch", "seq")


def flat_xor(value, mask):
    n = lax.axis_size("batch") * lax.axis_size("seq")
    return lax.ppermute(value, AXES, [(i, i ^ mask) for i in range(n)])


def log2(n):
    return n.bit_length() - 1


def gather_order(nb, ns, swap):
    seq_bits = list(range(log2(ns)))
    batch_bits = [log2(ns) + b for b in range(log2(nb))]
    low, mid, high = seq_bits[0], seq_bits[1], seq_bits[2:]
    cross = [mid] + batch_bits if not swap else batch_bits + [mid]
    return high[::-1] + cross + [low]


def my_flat():
    return lax.axis_index("batch") * lax.axis_size("seq") + lax.axis_index("seq")


def gather_rows(shard, swap):
    nb, ns = lax.axis_size("batch"), lax.axis_size("seq")
    nbits = log2(nb * ns)
    me = my_flat()
    shape = shard.shape
    buf = shard.reshape((1,) * nbits + shape)
    for bit in gather_order(nb, ns, swap):
        axis = nbits - 1 - bit
        other = flat_xor(buf, 1 << bit)
        mine = (me >> bit) & 1
        buf = jnp.where(
            mine == 1,
            jnp.concatenate([other, buf], axis),
            jnp.concatenate([buf, other], axis),
        )
    return buf.reshape((nb * ns * shape[0],) + shape[1:])


class Gather:
    def __init__(self, shard, swap):
        self.bits = gather_order(lax.axis_size("batch"), lax.axis_size("seq"), swap)
        self.order = tuple(self.bits[:-1])
        self.buf = shard.reshape((1,) + shard.shape[-2:])

    def step(self):
        other = flat_xor(self.buf, 1 << self.bits.pop(0))
        if self.bits:
            self.buf = jnp.concatenate([self.buf, other], axis=0)
        else:
            self.other = other
        return self.buf

    def rest(self):
        while self.bits:
            self.step()
        return self.buf, self.other


def slot(order, me, device):
    far = me ^ device
    at = (far >> order[0]) & 1
    for j in range(1, len(order)):
        at = at + (((far >> order[j]) & 1) << j)
    return at


class Scatter:
    def __init__(self, buf, swap, send=None):
        nbits = log2(lax.axis_size("batch") * lax.axis_size("seq"))
        self.bits = gather_order(lax.axis_size("batch"), lax.axis_size("seq"), swap)[::-1]
        self.send = send
        self.buf = buf if send is not None else buf.reshape((2,) * nbits + buf.shape[1:])
        self.tail = buf.shape[1:]
        self.nbits = nbits

    def step(self, beside=0.0):
        bit = self.bits.pop(0)
        axis = self.nbits - 1 - bit
        mine = (my_flat() >> bit) & 1
        if self.send is None:
            keep = lax.dynamic_index_in_dim(self.buf, mine, axis, True)
            send = lax.dynamic_index_in_dim(self.buf, 1 - mine, axis, True)
        else:
            keep, send, self.send = self.buf, self.send, None
        got = flat_xor(send, 1 << bit)
        buf = keep.astype(f32) + got.astype(f32) + beside
        if self.bits:
            buf = buf.astype(bf16)
        else:
            buf = buf.reshape(self.tail)
        if keep.ndim == 3 and self.bits:
            buf = buf.reshape((2,) * (self.nbits - 1) + (1,) + self.tail)
        self.buf = buf
        return buf

    def rest(self):
        while self.bits:
            self.step()
        return self.buf


def seq_perm(value, pairs):
    return lax.ppermute(value, "seq", pairs)


def exclusive_scan(tails, ids, rev, beside, final=lambda value: value):
    n = lax.axis_size("seq")
    place = lax.axis_index("seq")
    if rev:
        ids = ids[::-1]
    p = n - 1 - place if rev else place

    def at(q):
        return n - 1 - q if rev else q

    def move(value, pairs):
        return seq_perm(value, [(at(a), at(b)) for a, b in pairs])

    def gated(g, value):
        return g * value.astype(f32)

    c = p & 1
    x = (p >> 1) & 1
    base = p - (p & 3)
    pair = p - c
    seqs = tails.shape[0]
    rest = tails.shape[2:]
    wanted = [(pair, pair + 1), (base + 1, base + 3), (base - 1, base + 1), (pair - 1, pair)]
    step = 1
    while step * 4 < n:
        wanted += [(base + 3 - 4 * step, base - 1), (base + 3 - 4 * step, base + 3)]
        step *= 2
    where = jnp.stack([jnp.clip(t, 0, n - 1) for pair_of in wanted for t in pair_of])
    chosen = (where[:, None] == jnp.arange(n)[None, :]).astype(f32)
    keys = jnp.sum(chosen[:, :, None] * ids[None], axis=1)
    gates = (keys[0::2] == keys[1::2]).astype(f32)
    gates = jnp.broadcast_to(gates[:, :, None, None], gates.shape + (1, rest[-1]))
    gate_core, gate_pair, gate_plane, gate_entry = (gates[i] for i in range(4))
    parts = tails.reshape((seqs, 2, 2) + rest)

    def pick(a, i, axis):
        return lax.dynamic_index_in_dim(a, i, axis, False)

    core = [(i, i ^ 1) for i in range(n)]
    across = [(i, i ^ 2) for i in range(n)]
    own = pick(parts, c, 2)
    other = move(pick(parts, 1 - c, 2), core)
    first = jnp.where(c == 0, own, other)
    second = jnp.where(c == 0, other, own)
    pair_sum = second.astype(f32) + gated(gate_core[:, None], first)
    pair_mine = pick(pair_sum, x, 1)
    sent = pick(pair_sum, 1 - x, 1).astype(bf16)
    beside = beside(sent)
    pair_other = move(sent, across).astype(f32)
    low = jnp.where(x == 0, pair_mine, pair_other)
    high = jnp.where(x == 0, pair_other, pair_mine)
    total = high + gated(gate_pair, low)
    before = jnp.zeros_like(total)
    step = 1
    while step * 4 < n:
        total = total + (beside.pop(0) if beside else 0.0)
        got = move(
            total.astype(bf16), [(i, i + 4 * step) for i in range(n - 4 * step)]
        )
        at_step = 4 + 2 * log2(step)
        before = before + gated(gates[at_step], got)
        total = total + gated(gates[at_step + 1], got)
        step *= 2
    before_high = low + gated(gate_plane, before)
    mine = jnp.where(x == 0, before, before_high)
    theirs = jnp.where(x == 0, before_high, before) + sum(beside, jnp.zeros((1, 1), f32))
    got = move(theirs.astype(bf16), across)
    mine_b = mine.astype(bf16)
    entry = jnp.where(x == 0, jnp.stack([mine_b, got], 1), jnp.stack([got, mine_b], 1))
    after = first.astype(f32) + gated(gate_entry[:, None], entry)
    after_b = after.astype(bf16)
    mine = jnp.where(c == 0, entry, after_b)
    theirs = final(jnp.where(c == 0, after_b, entry))
    got = move(theirs, core)
    result = jnp.where(c == 0, jnp.stack([mine, got], 2), jnp.stack([got, mine], 2))
    return result.reshape(tails.shape)


NT = (((1,), (1,)), ((), ()))
VMEM_LIMIT = 56 * 1024 * 1024


def mm(a, b):
    return jnp.dot(a, b, preferred_element_type=f32)


def mm_nt(a, b):
    return lax.dot_general(a, b, NT, preferred_element_type=f32)


def lane_low(shape, half):
    return lax.broadcasted_iota(jnp.int32, shape, 1) < half


def half_sums(value, low):
    first = jnp.sum(jnp.where(low, value, 0.0), axis=1, keepdims=True)
    second = jnp.sum(jnp.where(low, 0.0, value), axis=1, keepdims=True)
    return first, second


def state_rows(ref, s, h, heads, d):
    per = heads // 4
    return ref[s, h // per, pl.ds((h % per) * d, d), :]


def total_rows(ref, s, heads, d):
    per = heads // 4
    out = []
    for q in range(4):
        rows = ref[s, q, pl.ds(per * d, 16), :].astype(f32)
        out += [rows[j : j + 1] for j in range(per)]
    return out


def pair_rows(first, second, core):
    return jnp.concatenate([first, second] if core == 0 else [second, first], axis=0)


def lay_out(pieces, width, out_ref):
    tiles = out_ref.shape[1] // 128
    lane = lax.broadcasted_iota(jnp.int32, (8, 128), 1)
    acc = [jnp.zeros((8, 128), f32)] * tiles
    for j, piece in enumerate(pieces):
        t, s = divmod(j * width, 128)
        turned = pltpu.roll(jnp.where(lane < width, piece, 0.0), s, 1) if s else jnp.where(lane < width, piece, 0.0)
        if s + width <= 128:
            acc[t] = acc[t] + turned
        else:
            acc[t] = acc[t] + jnp.where(lane >= s, turned, 0.0)
            acc[t + 1] = acc[t + 1] + jnp.where(lane < s, turned, 0.0)
    for t in range(tiles):
        out_ref[:, t * 128 : (t + 1) * 128] = acc[t]


def cut_out(values, width, count):
    tiles = values.shape[1] // 128
    lane = lax.broadcasted_iota(jnp.int32, (8, 128), 1)
    out = []
    for j in range(count):
        t, s = divmod(j * width, 128)
        piece = values[:, t * 128 : (t + 1) * 128]
        if s + width > 128:
            piece = jnp.where(lane >= s, piece, values[:, (t + 1) * 128 : (t + 2) * 128])
        out.append(pltpu.roll(piece, 128 - s, 1) if s else piece)
    return out


def fill_first(orders, shard_rows, piece, me_ref, wa_ref, wb_ref, bias, own_a, oth_a, own_b, oth_b, core):
    me = me_ref[0]
    unit = 2 * shard_rows
    count = wa_ref.shape[0] // unit

    def one(j, carry):
        rows = pl.ds(pl.multiple_of(j * unit, 16), unit)
        p = slot(orders[0], me, 2 * j)
        wa_ref[rows, :] = pair_rows(own_a[p], oth_a[p], core)
        p = slot(orders[1], me, 2 * j)
        wb_ref[rows, :] = pair_rows(own_b[p], oth_b[p], core)
        return carry

    lax.fori_loop(0, count, one, 0)
    first = wa_ref.shape[1] - 128
    pieces = []
    for j in range(count):
        two = wa_ref[j * unit : (j + 1) * unit, first:].astype(f32)
        pieces += [two[i * shard_rows : i * shard_rows + 8] for i in range(2)]
    lay_out(pieces, piece, bias)


def features_tiled_kernel(
    block, heads, d, orders, shard_rows, me_ref, x_ref, own_a, oth_a, own_b, oth_b, proj_ref, tg_ref,
    q_ref, k_ref, v_ref, phq_ref, phk_ref, tail_ref, wa_ref, wb_ref, z_scr, bias,
):
    @pl.when(pl.program_id(0) == 0)
    def _():
        piece = bias.shape[1] // (wa_ref.shape[0] // shard_rows)
        for core in range(2):
            pl.when(me_ref[0] % 2 == core)(
                partial(
                    fill_first, orders, shard_rows, piece, me_ref, wa_ref, wb_ref, bias,
                    own_a, oth_a, own_b, oth_b, core,
                )
            )

    features_kernel(
        block, heads, d, x_ref, wa_ref, wb_ref, bias, proj_ref, tg_ref,
        q_ref, k_ref, v_ref, phq_ref, phk_ref, tail_ref, z_scr,
    )


def features_kernel(
    block, heads, d, x_ref, wa_ref, wb_ref, b_ref, proj_ref, tg_ref,
    q_ref, k_ref, v_ref, phq_ref, phk_ref, tail_ref, z_scr,
):
    width = heads * d
    m = proj_ref.shape[2]
    pair = 2 * d
    scale = d ** (-0.25)
    root = m ** (-0.5)
    x = x_ref[...]
    rows = x.shape[0]
    low = lane_low((rows, pair), d)
    chunk = width // 2
    for t, (z_ref, ph_ref) in ((1, (k_ref, phk_ref)), (2, (v_ref, None)), (0, (q_ref, phq_ref))):
        for i in range(2):
            col = t * width + i * chunk
            w = wa_ref[:, col : col + chunk] if col < 3 * chunk else wb_ref[:, col - 3 * chunk : col - 2 * chunk]
            z = mm(x, w) + b_ref[0:1, col : col + chunk]
            z = (z * scale if ph_ref is not None else z).astype(bf16)
            z_ref[:, i * chunk : (i + 1) * chunk] = z
            if ph_ref is None:
                continue
            for p in range(chunk // pair):
                zp = z[:, p * pair : (p + 1) * pair]
                zf = zp.astype(f32)
                sums = half_sums(zf * zf, low)
                for e in range(2):
                    h = 2 * (i * (chunk // pair) + p) + e
                    u = mm(zp, proj_ref[h])
                    ph_ref[:, h * m : (h + 1) * m] = (jnp.exp(u - 0.5 * sums[e]) * root).astype(bf16)
    per = heads // 4
    for s in range(rows // block):
        r = slice(s * block, (s + 1) * block)
        tg = tg_ref[r, :].astype(bf16)
        for p in range(heads // 2):
            v_t = v_ref[r, p * pair : (p + 1) * pair].T
            for e in range(2):
                h = 2 * p + e
                kt = phk_ref[r, h * m : (h + 1) * m] * tg
                lhs = jnp.concatenate([v_t[e * d : (e + 1) * d], jnp.ones((16, block), bf16)], 0)
                res = mm(lhs, kt)
                tail_ref[s, h // per, pl.ds((h % per) * d, d), :] = res[:d].astype(bf16)
                z_scr[h % per : h % per + 1, :] = res[d : d + 1]
                if h % per == per - 1:
                    tail_ref[s, h // per, pl.ds(per * d, 16), :] = z_scr[...].astype(bf16)


def local_kernel(
    block, heads, d, phq_ref, phk_ref, v_ref, col_ref, row_ref, amat_ref, nd_ref, done_ref
):
    done_ref[...] = jnp.zeros_like(done_ref)
    m = phq_ref.shape[1] // heads
    pair = 2 * d
    low = lane_low((block, pair), d)
    t_ix = lax.broadcasted_iota(jnp.int32, (block, block), 0)
    j_ix = lax.broadcasted_iota(jnp.int32, (block, block), 1)
    causal = t_ix >= j_ix
    for s in range(v_ref.shape[0] // block):
        r = slice(s * block, (s + 1) * block)
        mask = jnp.logical_and(causal, col_ref[r, 0:1] == row_ref[s])
        for p in range(heads // 2):
            v_pair = v_ref[r, p * pair : (p + 1) * pair]
            for e in range(2):
                h = 2 * p + e
                sc = mm_nt(phq_ref[r, h * m : (h + 1) * m], phk_ref[r, h * m : (h + 1) * m])
                am = jnp.where(mask, sc, 0.0).astype(bf16)
                amat_ref[s, h] = am
                v_one = jnp.where(low if e == 0 else ~low, v_pair, jnp.ones_like(v_pair))
                nd_ref[r, h * pair : (h + 1) * pair] = mm(am, v_one)


def layer_norm(row_vals, gain, shift):
    inv = 1.0 / row_vals.shape[1]
    centred = row_vals - jnp.sum(row_vals, axis=1, keepdims=True) * inv
    rs = lax.rsqrt(jnp.sum(centred * centred, axis=1, keepdims=True) * inv + norm_eps)
    normed = centred * rs
    return normed * gain + shift, normed, rs


def layer_norm_back(dn, normed, rs):
    inv = 1.0 / dn.shape[1]
    mean = jnp.sum(dn, axis=1, keepdims=True) * inv
    proj = jnp.sum(dn * normed, axis=1, keepdims=True) * inv
    return rs * (dn - mean - normed * proj)


def group_rows(shard_rows):
    return math.lcm(shard_rows, 16) // shard_rows


def natural_rows(stage, out_ref, shard_rows, width):
    groups = stage.shape[1] // width
    per = group_rows(shard_rows)
    unit = per * shard_rows

    def one(i, carry):
        cols = [
            stage[pl.ds(pl.multiple_of(i * unit, 16), unit), g * width : (g + 1) * width]
            for g in range(groups)
        ]
        pieces = [c[j * shard_rows : (j + 1) * shard_rows] for j in range(per) for c in cols]
        out_ref[pl.ds(pl.multiple_of(i * unit * groups, 16), unit * groups), :] = jnp.concatenate(
            pieces, axis=0
        )
        return carry

    lax.fori_loop(0, stage.shape[0] // unit, one, 0)


def fill_rest(shard_rows, w_out_ref, vec_scr, b_in_scr, stage, vec_stage):
    width = w_out_ref.shape[1]
    natural_rows(stage, w_out_ref, shard_rows, width)
    unit = 2 * shard_rows
    pieces = []
    for j in range(vec_stage.shape[0] // unit):
        two = vec_stage[j * unit : (j + 1) * unit, :].astype(f32)
        pieces += [two[i * shard_rows : i * shard_rows + 8] for i in range(2)]
    lay_out(pieces, shard_rows, vec_scr)
    lay_out(pieces, w_out_ref.shape[0] // len(pieces), b_in_scr)


def middle_kernel(
    block, heads, d, ff_chunk,
    tiled, shard_rows, x_ref, cot_ref, phq_ref, nd_ref, pre_ref, gate_ref,
    *refs
):
    ins = refs[: 1 if tiled else 5]
    middle_parts(
        block, heads, d, ff_chunk, tiled, shard_rows, x_ref, cot_ref, phq_ref, nd_ref,
        pre_ref, gate_ref, ins, *refs[len(ins) :],
    )


def middle_parts(
    block, heads, d, ff_chunk, tiled, shard_rows, x_ref, cot_ref, phq_ref, nd_ref, pre_ref,
    gate_ref, ins,
    y_ref, dr1_ref, dnum_ref, dden_ref, dpre_ref, attn_ref, dao_ref, h1_ref, act_ref, dfo_ref,
    df_ref, sums_ref, sum_in_ref,
    attf, rden, dgel, z_scr, w_o_ref, w_in_ref, w_out_ref, vec_ref, b_in_ref, sems, *stages
):
    step = pl.program_id(0)
    m = phq_ref.shape[1] // heads
    width = heads * d
    ff = w_in_ref.shape[1]

    def copies():
        if tiled:
            cuts = [0, width, width + ff, width + 2 * ff, width + 2 * ff + 128]
            sources = [ins[0].at[:, i:j] for i, j in zip(cuts, cuts[1:])]
            places = (w_o_ref, w_in_ref) + tuple(stages)
        else:
            sources, places = ins, (w_o_ref, w_in_ref, w_out_ref, vec_ref, b_in_ref)
        return [
            pltpu.make_async_copy(src, dst, sems.at[i])
            for i, (src, dst) in enumerate(zip(sources, places))
        ]

    @pl.when(step == 0)
    def _():
        for c in copies():
            c.start()

    pair = 2 * d
    low = lane_low((block, pair), d)
    rows = x_ref.shape[0]
    seqs = rows // block
    ones = jnp.ones((d, 1), f32)
    for s in range(seqs):
        r = slice(s * block, (s + 1) * block)
        g = gate_ref[r, 2:3]
        zs = total_rows(pre_ref, s, heads, d)
        for p in range(heads // 2):
            tot = []
            for e in range(2):
                h = 2 * p + e
                st = state_rows(pre_ref, s, h, heads, d)
                zb = (ones * zs[h]).astype(bf16)
                rhs = jnp.concatenate([st, zb] if e == 0 else [zb, st], 0)
                tot.append(
                    nd_ref[r, h * pair : (h + 1) * pair]
                    + g * mm_nt(phq_ref[r, h * m : (h + 1) * m], rhs)
                )
            num = jnp.where(low, tot[0], tot[1])
            den = pltpu.roll(jnp.where(low, tot[1], tot[0]), d, 1)
            rd = 1.0 / den
            c = slice(p * pair, (p + 1) * pair)
            att = num * rd
            attf[r, c] = att
            rden[r, c] = rd
            attn_ref[r, c] = att.astype(bf16)

    @pl.when(step == 0)
    def _():
        for c in copies():
            c.wait()
        if tiled:
            fill_rest(shard_rows, w_out_ref, vec_ref, b_in_ref, *stages)

    b_o, gain1, shift1, b_out, gain2, shift2 = (vec_ref[i : i + 1, :] for i in range(6))
    r1 = x_ref[...].astype(f32) + mm(attn_ref[...], w_o_ref[...]) + b_o
    h1, n1, rs1 = layer_norm(r1, gain1, shift1)
    h1b = h1.astype(bf16)
    h1_ref[...] = h1b
    fo = None
    for c0 in range(0, ff, ff_chunk):
        c = slice(c0, c0 + ff_chunk)
        f = mm(h1b, w_in_ref[:, c]) + b_in_ref[6:7, c]
        phi = 0.5 + 0.5 * lax.erf(f * (0.5**0.5))
        act = (f * phi).astype(bf16)
        act_ref[:, c] = act
        dgel[:, c] = phi + f * (jnp.exp(-0.5 * f * f) * (1.0 / (2.0 * math.pi) ** 0.5))
        part = mm(act, w_out_ref[c, :])
        fo = part if fo is None else fo + part
    y, n2, rs2 = layer_norm(h1 + fo + b_out, gain2, shift2)
    y_ref[...] = y.astype(bf16)
    dy = cot_ref[...].astype(f32)

    def add_sum(i, value):
        row = jnp.sum(value, axis=0, keepdims=True)

        @pl.when(step == 0)
        def _():
            sums_ref[i : i + 1, :] = row

        @pl.when(step > 0)
        def _():
            sums_ref[i : i + 1, :] += row

    add_sum(4, dy * n2)
    add_sum(5, dy)
    dr2 = layer_norm_back(dy * gain2, n2, rs2)
    dfo = dr2.astype(bf16)
    dfo_ref[...] = dfo
    add_sum(3, dfo.astype(f32))
    dh1 = dr2
    for c0 in range(0, ff, ff_chunk):
        c = slice(c0, c0 + ff_chunk)
        df = (mm_nt(dfo, w_out_ref[c, :]) * dgel[:, c]).astype(bf16)
        df_ref[:, c] = df
        row = jnp.sum(df.astype(f32), axis=0, keepdims=True)

        @pl.when(step == 0)
        def _():
            sum_in_ref[:, c] = row

        @pl.when(step > 0)
        def _():
            sum_in_ref[:, c] += row

        dh1 = dh1 + mm_nt(df, w_in_ref[:, c])
    add_sum(1, dh1 * n1)
    add_sum(2, dh1)
    dr1 = layer_norm_back(dh1 * gain1, n1, rs1)
    dr1_ref[...] = dr1
    dao = dr1.astype(bf16)
    dao_ref[...] = dao
    add_sum(0, dao.astype(f32))
    dattn = mm_nt(dao, w_o_ref[...])
    dnum_ref[...] = (dattn * rden[...]).astype(bf16)
    prod = dattn * attf[...]
    lane = lax.broadcasted_iota(jnp.int32, (rows, 128), 1)
    low_rows = lane_low((rows, pair), d)
    dden = jnp.zeros((rows, 128), f32)
    for p in range(heads // 2):
        c = slice(p * pair, (p + 1) * pair)
        sums = half_sums(prod[:, c], low_rows)
        for e in range(2):
            col = -sums[e] * rden[:, p * pair + e * d : p * pair + e * d + 1]
            dden = jnp.where(lane == 2 * p + e, col, dden)
    dden = dden.astype(bf16).astype(f32)
    dden_ref[...] = dden
    per = heads // 4
    for s in range(seqs):
        r = slice(s * block, (s + 1) * block)
        g = gate_ref[r, 2:3]
        ddt = (dden[r] * g).T[:16].astype(bf16)
        for p in range(heads // 2):
            gdt = (dnum_ref[r, p * pair : (p + 1) * pair] * g.astype(bf16)).T
            for e in range(2):
                h = 2 * p + e
                lhs = jnp.concatenate([gdt[e * d : (e + 1) * d], ddt], 0)
                res = mm(lhs, phq_ref[r, h * m : (h + 1) * m])
                dpre_ref[s, h // per, pl.ds((h % per) * d, d), :] = res[:d].astype(bf16)
                z_scr[h % per : h % per + 1, :] = res[d + h : d + h + 1]
                if h % per == per - 1:
                    dpre_ref[s, h // per, pl.ds(per * d, 16), :] = z_scr[...].astype(bf16)


def back_query_kernel(
    block, heads, d,
    q_ref, v_ref, phq_ref, phk_ref, amat_ref, dnum_ref, dden_ref, pre_ref, gate_ref, row_ref,
    proj_ref,
    dq_ref, dv_ref, dsct_ref, done_ref,
):
    done_ref[...] = jnp.zeros_like(done_ref)
    m = phq_ref.shape[1] // heads
    pair = 2 * d
    scale = d ** (-0.25)
    low = lane_low((block, pair), d)
    t_ix = lax.broadcasted_iota(jnp.int32, (block, block), 0)
    j_ix = lax.broadcasted_iota(jnp.int32, (block, block), 1)
    causal = t_ix >= j_ix
    for s in range(q_ref.shape[0] // block):
        r = slice(s * block, (s + 1) * block)
        g = gate_ref[r, 2:3]
        gb = g.astype(bf16)
        mask = jnp.logical_and(causal, gate_ref[r, 0:1] == row_ref[s])
        zs = total_rows(pre_ref, s, heads, d)
        for p in range(heads // 2):
            c = slice(p * pair, (p + 1) * pair)
            dn = dnum_ref[r, c]
            v_pair = v_ref[r, c]
            qp = q_ref[r, c].astype(f32)
            st = jnp.concatenate(
                [state_rows(pre_ref, s, 2 * p, heads, d), state_rows(pre_ref, s, 2 * p + 1, heads, d)], 0
            )
            dv = None
            dq = None
            for e in range(2):
                h = 2 * p + e
                mine = low if e == 0 else ~low
                hm = slice(h * m, (h + 1) * m)
                dnm = jnp.where(mine, dn, jnp.zeros_like(dn))
                dd = dden_ref[r, h : h + 1]
                dsc = jnp.where(mask, mm_nt(dnm, v_pair) + dd, 0.0)
                dsct_ref[s, h] = dsc.T.astype(bf16)
                dph = mm(
                    jnp.concatenate([dsc.astype(bf16), dnm * gb], 1),
                    jnp.concatenate([phk_ref[r, hm], st], 0),
                ) + (g * dd) * zs[h]
                t = dph * phq_ref[r, hm].astype(f32)
                part = mm_nt(t.astype(bf16), proj_ref[h]) - jnp.where(
                    mine, jnp.sum(t, axis=1, keepdims=True) * qp, 0.0
                )
                dq = part if dq is None else dq + part
                part = mm(amat_ref[s, h].T, dnm)
                dv = part if dv is None else dv + part
            dq_ref[r, c] = (dq * scale).astype(bf16)
            dv_ref[r, c] = dv


def back_key_kernel(
    block, heads, d,
    k_ref, v_ref, phq_ref, phk_ref, dv_ref, dsct_ref, dtail_ref, gate_ref, proj_ref,
    dkv_ref,
):
    m = phq_ref.shape[1] // heads
    pair = 2 * d
    width = heads * d
    scale = d ** (-0.25)
    low = lane_low((block, pair), d)
    for s in range(k_ref.shape[0] // block):
        r = slice(s * block, (s + 1) * block)
        tg = gate_ref[r, 1:2]
        tgb = tg.astype(bf16)
        zs = total_rows(dtail_ref, s, heads, d)
        for p in range(heads // 2):
            c = slice(p * pair, (p + 1) * pair)
            v_pair = v_ref[r, c]
            kp = k_ref[r, c].astype(f32)
            ds = jnp.concatenate(
                [
                    state_rows(dtail_ref, s, 2 * p, heads, d),
                    state_rows(dtail_ref, s, 2 * p + 1, heads, d),
                ],
                0,
            )
            dk = None
            inter = []
            for e in range(2):
                h = 2 * p + e
                mine = low if e == 0 else ~low
                hm = slice(h * m, (h + 1) * m)
                vm = jnp.where(mine, v_pair, jnp.zeros_like(v_pair)) * tgb
                phk = phk_ref[r, hm]
                dph = mm(
                    jnp.concatenate([dsct_ref[s, h], vm], 1),
                    jnp.concatenate([phq_ref[r, hm], ds], 0),
                ) + tg * zs[h]
                t = dph * phk.astype(f32)
                part = mm_nt(t.astype(bf16), proj_ref[h]) - jnp.where(
                    mine, jnp.sum(t, axis=1, keepdims=True) * kp, 0.0
                )
                dk = part if dk is None else dk + part
                inter.append(mm_nt(phk, ds))
            dkv_ref[r, c] = (dk * scale).astype(bf16)
            dv = dv_ref[r, c] + tg * jnp.where(low, inter[0], inter[1])
            dkv_ref[r, width + p * pair : width + (p + 1) * pair] = dv.astype(bf16)


def params(micros):
    return dict(
        compiler_params=pltpu.CompilerParams(
            dimension_semantics=("arbitrary",), vmem_limit_bytes=VMEM_LIMIT
        ),
        cost_estimate=pl.CostEstimate(
            flops=int(micros * 8e9), bytes_accessed=int(micros * 1e6), transcendentals=0
        ),
    )


def row_spec(rows, cols):
    return pl.BlockSpec((rows, cols), lambda i: (i, 0))


def lead_spec(shape):
    return pl.BlockSpec(shape, lambda i: (i,) + (0,) * (len(shape) - 1))


def whole_spec(shape):
    return pl.BlockSpec(shape, lambda i: (0,) * len(shape))


def sds(shape, dtype):
    return jax.ShapeDtypeStruct(shape, dtype)


STEP_SEQS = 2
STATE_PAD = 16


def state_shape(seqs, heads, d, m):
    return (seqs, 4, heads // 4 * d + STATE_PAD, m)


def call_features(x, wa, wb, b, proj, tg, block, heads, d):
    rows, width = x.shape
    m = proj.shape[2]
    n = STEP_SEQS * block
    st = state_shape(STEP_SEQS, heads, d, m)
    return pl.pallas_call(
        partial(features_kernel, block, heads, d),
        grid=(rows // n,),
        in_specs=[
            row_spec(n, width), whole_spec(wa.shape), whole_spec(wb.shape), whole_spec(b.shape),
            whole_spec(proj.shape), row_spec(n, 1),
        ],
        out_specs=[row_spec(n, width)] * 3 + [row_spec(n, heads * m)] * 2 + [lead_spec(st)],
        out_shape=[sds((rows, width), bf16)] * 3
        + [sds((rows, heads * m), bf16)] * 2
        + [sds((rows // block,) + st[1:], bf16)],
        scratch_shapes=[pltpu.VMEM((16, m), f32)],
        name="features",
        **params(10),
    )(x, wa, wb, b, proj, tg)


def call_features_tiled(x, a, b, proj, tg, shard_rows, block, heads, d):
    rows, width = x.shape
    m = proj.shape[2]
    n = STEP_SEQS * block
    st = state_shape(STEP_SEQS, heads, d, m)
    parts = (a.buf, a.other, b.buf, b.other)
    wa, wb = (width, a.buf.shape[2]), (width, b.buf.shape[2])
    return pl.pallas_call(
        partial(features_tiled_kernel, block, heads, d, (a.order, b.order), shard_rows),
        grid=(rows // n,),
        in_specs=[pl.BlockSpec(memory_space=pltpu.SMEM), row_spec(n, width)]
        + [whole_spec(t.shape) for t in parts]
        + [whole_spec(proj.shape), row_spec(n, 1)],
        out_specs=[row_spec(n, width)] * 3
        + [row_spec(n, heads * m)] * 2
        + [lead_spec(st), whole_spec(wa), whole_spec(wb)],
        out_shape=[sds((rows, width), bf16)] * 3
        + [sds((rows, heads * m), bf16)] * 2
        + [sds((rows // block,) + st[1:], bf16), sds(wa, bf16), sds(wb, bf16)],
        scratch_shapes=[pltpu.VMEM((16, m), f32), pltpu.VMEM((8, 3 * width), f32)],
        name="features",
        **params(12),
    )(my_flat().astype(jnp.int32).reshape(1), x, *parts, proj, tg)


def call_local(phq, phk, v, gates, id_rows, block, heads, d):
    rows = v.shape[0]
    n = STEP_SEQS * block
    return pl.pallas_call(
        partial(local_kernel, block, heads, d),
        grid=(rows // n,),
        in_specs=[
            row_spec(n, phq.shape[1]), row_spec(n, phk.shape[1]), row_spec(n, v.shape[1]),
            row_spec(n, gates.shape[1]), lead_spec((STEP_SEQS, 1, block)),
        ],
        out_specs=[
            lead_spec((STEP_SEQS, heads, block, block)), row_spec(n, heads * 2 * d),
            whole_spec((1, 1)),
        ],
        out_shape=[
            sds((rows // block, heads, block, block), bf16), sds((rows, heads * 2 * d), f32),
            sds((1, 1), f32),
        ],
        name="local",
        **params(8),
    )(phq, phk, v, gates, id_rows)


def call_middle(x, cot, phq, nd, pre, gates, weights, tiled, shard_rows, ff, block, heads, d):
    rows, width = x.shape
    m = phq.shape[1] // heads
    n = STEP_SEQS * block
    st = (STEP_SEQS,) + pre.shape[1:]
    return pl.pallas_call(
        partial(middle_kernel, block, heads, d, 768, tiled, shard_rows),
        grid=(rows // n,),
        in_specs=[
            row_spec(n, width), row_spec(n, width), row_spec(n, phq.shape[1]),
            row_spec(n, nd.shape[1]), lead_spec(st), row_spec(n, gates.shape[1]),
        ]
        + [pl.BlockSpec(memory_space=pl.ANY)] * len(weights),
        out_specs=[
            row_spec(n, width), row_spec(n, width), row_spec(n, width), row_spec(n, 128),
            lead_spec(st), row_spec(n, width), row_spec(n, width), row_spec(n, width),
            row_spec(n, ff), row_spec(n, width), row_spec(n, ff), whole_spec((8, width)),
            whole_spec((1, ff)),
        ],
        out_shape=[
            sds((rows, width), bf16), sds((rows, width), f32), sds((rows, width), bf16),
            sds((rows, 128), f32), sds(pre.shape, bf16), sds((rows, width), bf16),
            sds((rows, width), bf16), sds((rows, width), bf16), sds((rows, ff), bf16),
            sds((rows, width), bf16), sds((rows, ff), bf16), sds((8, width), f32),
            sds((1, ff), f32),
        ],
        scratch_shapes=[
            pltpu.VMEM((n, width), f32), pltpu.VMEM((n, width), f32), pltpu.VMEM((n, ff), f32),
            pltpu.VMEM((16, m), f32), pltpu.VMEM((width, width), bf16),
            pltpu.VMEM((width, ff), bf16), pltpu.VMEM((ff, width), bf16),
            pltpu.VMEM((8, width), f32), pltpu.VMEM((8, ff), f32), pltpu.SemaphoreType.DMA((5,)),
        ]
        + ([pltpu.VMEM((width, ff), bf16), pltpu.VMEM((width, 128), bf16)] if tiled else []),
        name="middle",
        **params(31),
    )(x, cot, phq, nd, pre, gates, *weights)


def call_back_query(
    half, q, v, phq, phk, amat, dnum, dden, pre, gates, id_rows, proj, ties, block, heads, d
):
    rows, width = q.shape
    n = STEP_SEQS * block
    sq = (STEP_SEQS, heads, block, block)

    def rs(cols):
        return pl.BlockSpec((n, cols), lambda i: (half, 0))

    def ls(shape):
        return pl.BlockSpec(shape, lambda i: (half,) + (0,) * (len(shape) - 1))

    def kernel(*refs):
        back_query_kernel(block, heads, d, *refs[:11], *refs[11 + len(ties) :])

    return pl.pallas_call(
        kernel,
        grid=(1,),
        in_specs=[
            rs(width), rs(width), rs(phq.shape[1]), rs(phk.shape[1]), ls(sq), rs(width), rs(128),
            ls((STEP_SEQS,) + pre.shape[1:]), rs(gates.shape[1]), ls((STEP_SEQS, 1, block)),
            whole_spec(proj.shape),
        ]
        + [pl.BlockSpec(memory_space=pl.ANY)] * len(ties),
        out_specs=[row_spec(n, width), row_spec(n, width), lead_spec(sq), whole_spec((1, 1))],
        out_shape=[
            sds((n, width), bf16), sds((n, width), f32), sds(sq, bf16), sds((1, 1), f32),
        ],
        name="back_query",
        **params(8),
    )(q, v, phq, phk, amat, dnum, dden, pre, gates, id_rows, proj, *ties)


def call_back_key(k, v, phq, phk, dvs, dscts, dtail, gates, proj, ties, block, heads, d):
    rows, width = k.shape
    n = STEP_SEQS * block
    sq = (STEP_SEQS, heads, block, block)
    steps = rows // n

    def kernel(k_ref, v_ref, phq_ref, phk_ref, *refs):
        for i in range(steps):

            @pl.when(pl.program_id(0) == i)
            def _():
                back_key_kernel(
                    block, heads, d, k_ref, v_ref, phq_ref, phk_ref, refs[i], refs[steps + i],
                    *refs[2 * steps : 2 * steps + 3], refs[-1],
                )

    return pl.pallas_call(
        kernel,
        grid=(steps,),
        in_specs=[
            row_spec(n, width), row_spec(n, width), row_spec(n, phq.shape[1]),
            row_spec(n, phk.shape[1]),
        ]
        + [whole_spec((n, width))] * steps
        + [whole_spec(sq)] * steps
        + [
            lead_spec((STEP_SEQS,) + dtail.shape[1:]), row_spec(n, gates.shape[1]),
            whole_spec(proj.shape),
        ]
        + [pl.BlockSpec(memory_space=pl.ANY)] * len(ties),
        out_specs=row_spec(n, 2 * width),
        out_shape=sds((rows, 2 * width), bf16),
        name="back_key",
        **params(13),
    )(k, v, phq, phk, *dvs, *dscts, dtail, gates, proj, *ties)


TN = (((0,), (0,)), ((), ()))


def mm_tn(a, b):
    return lax.dot_general(a, b, TN, preferred_element_type=f32)


def pack_kernel(shard_rows, w_o_ref, w_in_ref, w_out_ref, vec_ref, *refs):
    out_ref = refs[-1]
    rows = w_out_ref[...]
    parts = [w_o_ref[...], w_in_ref[...]]
    parts += [rows[i : i + shard_rows] for i in range(0, rows.shape[0], shard_rows)]
    parts += [vec_ref[...]]
    at = 0
    for part in parts:
        out_ref[:, at : at + part.shape[1]] = part
        at += part.shape[1]


def call_pack(w_o, w_in, w_out, vec, ties):
    rows = w_o.shape[0]
    cols = (w_o.size + w_in.size + w_out.size + vec.size) // rows
    return pl.pallas_call(
        partial(pack_kernel, rows),
        in_specs=[pl.BlockSpec(memory_space=pltpu.VMEM)] * 4
        + [pl.BlockSpec(memory_space=pl.ANY)] * len(ties),
        out_shape=sds((rows, cols), bf16),
        name="pack",
    )(w_o, w_in, w_out, vec, *ties)


def part_store(core, refs, index, value):
    kept, sent, rows, cols = refs
    (kept if index % 2 == core else sent)[index // 2, rows, cols] = value


def by_core(kernel, core_ref):
    for core in range(2):
        pl.when(core_ref[0] == core)(partial(kernel, core))


def grads_kernel(
    shard_rows, core_ref, attn_ref, dao_ref, h1_ref, df_ref, act_ref, dfo_ref, sums_ref, sum_in_ref,
    tie_ref, keep_i, send_i, keep_o, send_o, done_ref,
):
    done_ref[...] = jnp.zeros_like(done_ref)
    by_core(
        partial(
            grads_parts, shard_rows, attn_ref, dao_ref, h1_ref, df_ref, act_ref, dfo_ref, sums_ref,
            sum_in_ref, keep_i, send_i, keep_o, send_o,
        ),
        core_ref,
    )


def grads_parts(
    shard_rows, attn_ref, dao_ref, h1_ref, df_ref, act_ref, dfo_ref, sums_ref, sum_in_ref,
    keep_i, send_i, keep_o, send_o, core,
):
    width = dao_ref.shape[1]
    ff = df_ref.shape[1]
    groups = ff // width
    tall = groups * shard_rows
    count = h1_ref.shape[1] // shard_rows
    every = slice(None)
    dfo = dfo_ref[...]
    chunk = act_ref.shape[1] // groups
    per = chunk // tall
    for c in range(groups):
        res = mm_tn(act_ref[:, c * chunk : (c + 1) * chunk], dfo).astype(bf16)
        for j in range(per):
            part_store(
                core, (keep_o, send_o, slice(0, tall), every), c * per + j,
                res[j * tall : (j + 1) * tall],
            )
    res = mm_tn(attn_ref[...], dao_ref[...]).astype(bf16)
    for j in range(count):
        part_store(
            core, (keep_o, send_o, slice(tall, tall + shard_rows), every), j,
            res[j * shard_rows : (j + 1) * shard_rows],
        )
    h1 = h1_ref[...]
    for g in range(groups):
        res = mm_tn(h1, df_ref[:, g * width : (g + 1) * width]).astype(bf16)
        for j in range(count):
            part_store(
                core, (keep_i, send_i, every, slice(g * width, (g + 1) * width)), j,
                res[j * shard_rows : (j + 1) * shard_rows],
            )
    step = pl.program_id(0)
    small = cut_out(sums_ref[...], shard_rows, 2 * count)
    large = cut_out(jnp.broadcast_to(sum_in_ref[...], (8, ff)), groups * shard_rows, 2 * count)
    row = lax.broadcasted_iota(jnp.int32, (8, 128), 0)
    for j in range(count):
        a = jnp.where(step == 0, small[j], small[j + count])
        b = jnp.where(step == 0, large[j], large[j + count])
        value = jnp.concatenate(
            [jnp.where(row == 6, b, a), jnp.zeros((shard_rows - 8, 128), f32)], axis=0
        )
        part_store(core, (keep_i, send_i, every, slice(ff, ff + 128)), j, value.astype(bf16))


def call_grads(core, attn, dao, h1, df, act, dfo, sums, sum_in, tie, shard_rows):
    rows, width = dao.shape
    ff = df.shape[1]
    steps = 2
    n_dev = width // shard_rows
    small = (n_dev // 2, shard_rows, ff + 128)
    tall = (n_dev // 2, shard_rows * (ff // width + 1), width)

    def cut(shape):
        return lead_spec((shape[0] // steps,) + shape[1:])

    return pl.pallas_call(
        partial(grads_kernel, shard_rows),
        grid=(steps,),
        in_specs=[
            pl.BlockSpec(memory_space=pltpu.SMEM),
            pl.BlockSpec((rows, width // steps), lambda i: (0, i)), whole_spec(dao.shape),
            pl.BlockSpec((rows, width // steps), lambda i: (0, i)), whole_spec(df.shape),
            pl.BlockSpec((rows, ff // steps), lambda i: (0, i)), whole_spec(dfo.shape),
            whole_spec(sums.shape), whole_spec(sum_in.shape),
            pl.BlockSpec(memory_space=pl.ANY),
        ],
        out_specs=[cut(small), cut(small), cut(tall), cut(tall), whole_spec((1, 1))],
        out_shape=[sds(small, bf16), sds(small, bf16), sds(tall, bf16), sds(tall, bf16)]
        + [sds((1, 1), f32)],
        name="grads",
        **params(10),
    )(core, attn, dao, h1, df, act, dfo, sums, sum_in, tie)


def first_grads_kernel(
    shard_rows, ties, core_ref, x_ref, dq_ref, dkv_ref, *refs
):
    by_core(partial(first_grads_parts, shard_rows, x_ref, dq_ref, dkv_ref, *refs[ties:]), core_ref)


def first_grads_parts(
    shard_rows, x_ref, dq_ref, dkv_ref, keep_a, send_a, keep_b, send_b, core
):
    width = dq_ref.shape[1]
    chunk = width // 2
    x = x_ref[...]
    step = pl.program_id(0)
    count = x_ref.shape[1] // shard_rows
    n_dev = 2 * count
    every = slice(None)
    sums = []
    for i in range(6):
        src, c0 = (dq_ref, i * chunk) if i < 2 else (dkv_ref, (i - 2) * chunk)
        b = src[:, c0 : c0 + chunk]
        sums.append(jnp.sum(b.astype(f32), axis=0, keepdims=True))
        res = mm_tn(x, b).astype(bf16)
        refs = (keep_a, send_a) if i < 3 else (keep_b, send_b)
        cols = slice((i % 3) * chunk, (i % 3 + 1) * chunk)
        for j in range(count):
            part_store(core, refs + (every, cols), j, res[j * shard_rows : (j + 1) * shard_rows])
    row = jnp.broadcast_to(jnp.concatenate(sums, axis=1), (8, 3 * width))
    pieces = cut_out(row, 3 * width // n_dev, n_dev)
    for j in range(count):
        value = jnp.concatenate(
            [
                jnp.where(step == 0, pieces[j], pieces[j + count]),
                jnp.zeros((shard_rows - 8, 128), f32),
            ],
            axis=0,
        )
        cols = slice(3 * chunk, 3 * chunk + 128)
        part_store(core, (keep_a, send_a, every, cols), j, value.astype(bf16))


def call_first_grads(core, x, dq, dkv, ties, shard_rows):
    rows, width = x.shape
    steps = 2
    half = 3 * width // 2
    n_dev = width // shard_rows
    shapes = [(n_dev // 2, shard_rows, half + 128)] * 2 + [(n_dev // 2, shard_rows, half)] * 2
    return pl.pallas_call(
        partial(first_grads_kernel, shard_rows, len(ties)),
        grid=(steps,),
        in_specs=[
            pl.BlockSpec(memory_space=pltpu.SMEM),
            pl.BlockSpec((rows, width // steps), lambda i: (0, i)), whole_spec(dq.shape),
            whole_spec(dkv.shape),
        ]
        + [pl.BlockSpec(memory_space=pl.ANY)] * len(ties),
        out_specs=[lead_spec((t[0] // steps,) + t[1:]) for t in shapes],
        out_shape=[sds(t, bf16) for t in shapes],
        name="first_grads",
        **params(6),
    )(core, x, dq, dkv, *ties)


def input_grad_kernel(dq_ref, dkv_ref, wa_ref, wb_ref, dr1_ref, *refs):
    out_ref, done_ref = refs[-2:]
    done_ref[...] = jnp.zeros_like(done_ref)
    width = dq_ref.shape[1]
    chunk = width // 2
    acc = dr1_ref[...]
    for i in range(6):
        src, c0 = (dq_ref, i * chunk) if i < 2 else (dkv_ref, (i - 2) * chunk)
        w_ref = wa_ref if i < 3 else wb_ref
        acc = acc + mm_nt(src[:, c0 : c0 + chunk], w_ref[:, (i % 3) * chunk : (i % 3 + 1) * chunk])
    out_ref[...] = acc.astype(bf16)


def call_input_grad(dq, dkv, wa, wb, dr1, ties, n):
    rows, width = dq.shape
    return pl.pallas_call(
        input_grad_kernel,
        grid=(rows // n,),
        in_specs=[
            row_spec(n, width), row_spec(n, 2 * width), whole_spec(wa.shape), whole_spec(wb.shape),
            row_spec(n, width),
        ]
        + [pl.BlockSpec(memory_space=pl.ANY)] * len(ties),
        out_specs=[row_spec(n, width), whole_spec((1, 1))],
        out_shape=[sds((rows, width), bf16), sds((1, 1), f32)],
        name="input_grad",
        **params(6),
    )(dq, dkv, wa, wb, dr1, *ties)


def body(
    inputs,
    seg_ids,
    cotangent,
    projection,
    w_qkv,
    b_qkv,
    w_o,
    b_o,
    ln1_gain,
    ln1_bias,
    w_in,
    b_in,
    w_out,
    b_out,
    ln2_gain,
    ln2_bias,
):
    micro, seqs_micro, block, width = inputs.shape
    heads, d, m = projection.shape
    n_seq = lax.axis_size("seq")
    n_dev = lax.axis_size("batch") * n_seq
    place = lax.axis_index("seq")
    seqs = micro * seqs_micro
    rows = seqs * block

    vectors = (b_qkv, b_o, ln1_gain, ln1_bias, b_in, b_out, ln2_gain, ln2_bias)
    sizes = [v.shape[0] for v in vectors]
    cuts = [sum(sizes[:i]) for i in range(len(sizes) + 1)]
    idents = seg_ids.reshape(seqs, block)
    shard_rows = w_qkv.shape[0]
    tiled = shard_rows % 8 == 0
    ids_b = idents[:, -1].astype(bf16)

    def as_rows(parts):
        t = jnp.stack([jnp.pad(t, (0, 128 - t.shape[0])) for t in parts])
        return jnp.pad(t, ((0, shard_rows - len(parts)), (0, 0)))

    order = (1, 2, 3, 5, 6, 7, 4)
    half = w_qkv.shape[1] // 2
    x = inputs.reshape(rows, width)
    dims = (block, heads, d)
    idents_f = idents.astype(f32)
    tail_gate = (idents_f == idents_f[:, -1:]).astype(f32)
    zero = jnp.zeros_like(projection[::2])
    proj = jnp.stack(
        [
            jnp.concatenate([projection[0::2], zero], axis=1),
            jnp.concatenate([zero, projection[1::2]], axis=1),
        ],
        axis=1,
    ).reshape(heads, 2 * d, m)
    f_cols = w_in.shape[1]
    if tiled:
        first = jnp.concatenate([w_qkv[:, :half], as_rows((b_qkv, ids_b))], axis=1)
        gather_a, gather_b = Gather(first, False), Gather(w_qkv[:, half:], True)
        ties = ()
        for _ in range(1):
            ties = (gather_a.step(), gather_b.step())
        packed = call_pack(w_o, w_in, w_out, as_rows([vectors[i] for i in order]), ties)
        gather_a.rest()
        gather_b.rest()
        weights = (lax.all_gather(packed, AXES, axis=0, tiled=True),)
        ids = jnp.concatenate([t[:, 1, half : half + seqs] for t in (gather_a.buf, gather_a.other)])
        device = lax.axis_index("batch") * n_seq + jnp.arange(n_seq)
        index = slot(gather_a.order, my_flat(), device) + ((device ^ my_flat()) & 1) * (n_dev // 2)
        chosen = (index[:, None] == jnp.arange(n_dev)[None, :]).astype(f32)
        last_all = jnp.sum(chosen[:, :, None] * ids.astype(f32)[None], axis=1)
        q, k, v, phq, phk, tails, w_a, w_b = call_features_tiled(
            x, gather_a, gather_b, proj, tail_gate.reshape(rows, 1), shard_rows, *dims
        )
    else:
        flat = jnp.concatenate(vectors + (ids_b,))
        flat = jnp.pad(flat, (0, -flat.shape[0] % 128)).reshape(-1, 128)
        used = flat.shape[0]
        flat = jnp.pad(flat, ((0, shard_rows - used), (0, 0)))
        w_a = gather_rows(jnp.concatenate([w_qkv[:, :half], flat], axis=1), False)
        w_b = gather_rows(w_qkv[:, half:], True)
        packed = w_a[:, half:].reshape(n_dev, shard_rows, 128)[:, :used].reshape(n_dev, -1)
        whole = [
            packed[:, cuts[i] : cuts[i] + sizes[i]].reshape(1, -1).astype(f32)
            for i in range(len(sizes))
        ]
        ids_all = packed[:, cuts[-1] : cuts[-1] + seqs].reshape(-1, n_seq, seqs).astype(f32)
        last_all = lax.dynamic_index_in_dim(ids_all, lax.axis_index("batch"), 0, False)
        rows_of = [whole[i] for i in order[:6]]
        weights = (
            gather_rows(w_o, False), gather_rows(w_in, True), gather_rows(w_out, False),
            jnp.concatenate(rows_of + rows_of[:2]), jnp.concatenate([whole[4]] * 8),
        )
        q, k, v, phq, phk, tails = call_features(
            x, w_a, w_b, whole[0], proj, tail_gate.reshape(rows, 1), *dims
        )

    pre_all = jnp.concatenate([-jnp.ones_like(last_all[:1]), last_all[:-1]], axis=0)
    pre_ident = lax.dynamic_index_in_dim(pre_all, place, 0, False)
    gates = jnp.stack(
        [
            idents_f,
            tail_gate,
            (idents_f == pre_ident[:, None]).astype(f32),
        ],
        axis=-1,
    ).reshape(rows, 3)
    gates = jnp.pad(gates, ((0, 0), (0, 5)))
    id_rows = idents_f[:, None, :]
    amat, nd, done = call_local(phq, phk, v, gates, id_rows, *dims)
    pre = exclusive_scan(tails, last_all, False, lambda sent: [done])
    (y, dr1, dnum, dden, dpre, attn, dao, h1, act, dfo, df, sums, sum_in) = call_middle(
        x, cotangent.reshape(rows, width), phq, nd, pre, gates, weights, tiled,
        shard_rows, f_cols, *dims,
    )
    core = (place & 1).astype(jnp.int32).reshape(1)

    def grad(a, b):
        return mm_tn(a, b).astype(bf16)

    halves, scatters = [], []

    def run_beside(sent):
        zeros = []
        if tiled:
            keep_i, send_i, keep_o, send_o, done = call_grads(
                core, attn, dao, h1, df, act, dfo, sums, sum_in, sent, shard_rows
            )
            zeros = [0.0]
            wide, tall = (keep_i, True, send_i), (keep_o, False, send_o)
        else:
            pieces = [t.reshape(n_dev, -1) for t in [sums[i] for i in range(6)] + [sum_in[0]]]
            vec = jnp.concatenate(pieces, axis=1)
            vec = jnp.pad(vec, ((0, 0), (0, -vec.shape[1] % 128))).reshape(n_dev, -1, 128)
            vec = jnp.pad(vec, ((0, 0), (0, shard_rows - vec.shape[1]), (0, 0))).astype(bf16)
            wide = jnp.concatenate([grad(h1, df).reshape(n_dev, shard_rows, -1), vec], axis=2)
            tall = [grad(act, dfo).reshape(n_dev, -1, width), grad(attn, dao).reshape(n_dev, -1, width)]
            wide, tall = (wide, True), (jnp.concatenate(tall, axis=1), False)
        scatters.append(Scatter(*wide))
        scatters.append(Scatter(*tall))
        for i in range(seqs // STEP_SEQS):
            halves.append(
                call_back_query(
                    i, q, v, phq, phk, amat, dnum, dden, pre, gates, id_rows, proj,
                    (), *dims
                )
            )
        return zeros + [t[3] for t in halves]

    def start_scatters(value):
        first = [t.step() for t in scatters]
        value, *first = lax.optimization_barrier((value, *first))
        for t, buf in zip(scatters, first):
            t.buf = buf
        return value

    back = exclusive_scan(dpre, pre_all, True, run_beside, start_scatters)
    scatter_i, scatter_o = scatters
    dqs, dvs, dscts, dones = zip(*halves)
    dq = jnp.concatenate(dqs)
    ties = ()
    dkv = call_back_key(k, v, phq, phk, dvs, dscts, back, gates, proj, ties, *dims)
    ties = ()
    if tiled:
        keep_a, send_a, keep_b, send_b = call_first_grads(core, x, dq, dkv, ties, shard_rows)
        scatter_a = Scatter(keep_a, False, send_a)
        scatter_b = Scatter(keep_b, True, send_b)
    else:
        dqkv = jnp.concatenate([dq, dkv], axis=1)
        gw = grad(x, dqkv).reshape(n_dev, shard_rows, -1)
        vec = jnp.sum(dqkv, axis=0, dtype=f32).reshape(n_dev, 1, -1)
        vec = jnp.pad(vec, ((0, 0), (0, shard_rows - 1), (0, 128 - sizes[0]))).astype(bf16)
        scatter_a = Scatter(jnp.concatenate([gw[:, :, :half], vec], axis=2), False)
        scatter_b = Scatter(gw[:, :, half:], True)
    ties = (scatter_a.step(), scatter_b.step()) + (scatter_i.step(), scatter_o.step())
    dx, done = call_input_grad(dq, dkv, w_a, w_b, dr1, ties, STEP_SEQS * block)
    scatter_a.step(done)
    scatter_b.step()
    part_a = scatter_a.rest()
    part_b = scatter_b.rest()
    part_i = scatter_i.rest()
    part_o = scatter_o.rest()
    g_w_out, g_w_o = part_o[: w_out.shape[0]], part_o[w_out.shape[0] :]
    g_w_in = part_i[:, :f_cols]
    lengths = [sizes[i] for i in order]
    if tiled:
        vec_grads = [part_i[i, f_cols : f_cols + n] for i, n in enumerate(lengths)]
    else:
        vec = part_i[:, f_cols:].reshape(-1)
        starts = [sum(lengths[:i]) for i in range(len(lengths))]
        vec_grads = [vec[at : at + n] for at, n in zip(starts, lengths)]
    (g_b_o, g_gain_one, g_shift_one, g_b_out, g_gain_two, g_shift_two, g_b_in) = vec_grads
    g_w_qkv = jnp.concatenate([part_a[:, :half], part_b], axis=1)
    g_b_qkv = part_a[0, half : half + sizes[0]]
    return (
        y.reshape(inputs.shape),
        dx.reshape(inputs.shape),
        g_w_qkv,
        g_b_qkv,
        g_w_o,
        g_b_o,
        g_gain_one,
        g_shift_one,
        g_w_in,
        g_b_in,
        g_w_out,
        g_b_out,
        g_gain_two,
        g_shift_two,
    )


def solution(mesh):
    rows = P(AXES, None)
    vec = P(AXES)
    tok = P(None, "batch", "seq", None)
    in_specs = (
        tok,
        P(None, "batch", "seq"),
        tok,
        P(),
        rows,
        vec,
        rows,
        vec,
        vec,
        vec,
        rows,
        vec,
        rows,
        vec,
        vec,
        vec,
    )
    out_specs = (tok, tok, rows, vec, rows, vec, vec, vec, rows, vec, rows, vec, vec, vec)
    return jax.shard_map(body, mesh=mesh, in_specs=in_specs, out_specs=out_specs, check_vma=False)
```

profile of v0, /device:TPU:0, one launch (start us, length us, event | category | flops | bytes accessed | tf_op | source)
XLA Modules:
  0.0 372.1 jit_solution(14856793115817588186)
XLA Ops:
  36.7 10.6 %collective-permute-done.3 = bf16[8,24,1280]{2,1,0:T(8,128)(2,1)S(1)} collective-permute-done((bf16[8,24,1280]{2,1,0:T(8,128)(2,1)S(1)}, bf16[8,24,1280]{2,1,0:T(8,128)(2,1)S(1)}, u32[]{:S(2)}, u32[]{:S(2)}) %collective-permute-start.3) | collective-permute-done | bytes 491552 | tf_op jit(solution)/shard_map/ppermute | solution.py:19
  53.6 12.5 %features.1 = (bf16[512,768]{1,0:T(8,128)(2,1)}, bf16[512,768]{1,0:T(8,128)(2,1)}, bf16[512,768]{1,0:T(8,128)(2,1)}, bf16[512,3072]{1,0:T(8,128)(2,1)}, bf16[512...) custom-call(s32[1]{0:T(128)} %bitcast.2.me_ref, ...), custom_call_target="tpu_custom_call" | custom-call | flops 96000000000 | bytes 12000000 | tf_op jit(solution)/shard_map/features/pallas_call | solution.py:767
  72.7 8.3 %local.1 = (bf16[4,12,128,128]{3,2,1,0:T(8,128)(2,1)}, f32[512,1536]{1,0:T(8,128)}, f32[1,1]{1,0:T(1,128)}) custom-call(bf16[512,3072]{1,0:T(8,128)(2,1)} %get-tuple-element.59.phq_ref.refs_2_, bf16[512,3072]{1,0:T(8,128)(2,1)} %get-tuple-element.60.phk_ref.refs_3_, bf16[512,768]{1,0:T(8,128)(2,1)} %get-tuple-element.61.v_ref.refs_1_, ...), custom_call_target="tpu_custom_call" | custom-call | flops 64000000000 | bytes 8000000 | tf_op jit(solution)/shard_map/local/pallas_call | solution.py:788
  81.0 5.9 %collective-permute-done.11 = bf16[4,208,256]{2,1,0:T(8,128)(2,1)S(1)} collective-permute-done((bf16[4,208,256]{2,1,0:T(8,128)(2,1)S(1)}, bf16[4,208,256]{2,1,0:T(8,128)(2,1)S(1)}, u32[]{:S(2)}, u32[]{:S(2)}) %collective-permute-start.11) | collective-permute-done | bytes 426016 | tf_op jit(solution)/shard_map/ppermute | solution.py:120
  91.1 18.3 %collective-permute-done.12 = bf16[4,208,256]{2,1,0:T(8,128)(2,1)S(1)} collective-permute-done((bf16[4,208,256]{2,1,0:T(8,128)(2,1)S(1)}, bf16[4,208,256]{2,1,0:T(8,128)(2,1)S(1)}, u32[]{:S(2)}, u32[]{:S(2)}) %collective-permute-start.12) | collective-permute-done | bytes 426016 | tf_op jit(solution)/shard_map/ppermute | solution.py:120
  110.3 13.3 %collective-permute-start.13 = (bf16[4,208,256]{2,1,0:T(8,128)(2,1)S(1)}, bf16[4,208,256]{2,1,0:T(8,128)(2,1)S(1)}, u32[]{:S(2)}, u32[]{:S(2)}) collective-permute-start(bf16[4,208,256]{2,1,0:T(8,128)(2,1)S(1)} %fusion.12), channel_id=1, source_target_pairs={{0,8},{1,9},{2,10},{3,11},{4,12},{5,13},{6,14},{7,15},{16,24},{17,... | collective-permute-start | bytes 1277960 | tf_op jit(solution)/shard_map/ppermute | solution.py:120
  123.6 5.2 %collective-permute-done.13 = bf16[4,208,256]{2,1,0:T(8,128)(2,1)S(1)} collective-permute-done((bf16[4,208,256]{2,1,0:T(8,128)(2,1)S(1)}, bf16[4,208,256]{2,1,0:T(8,128)(2,1)S(1)}, u32[]{:S(2)}, u32[]{:S(2)}) %collective-permute-start.13) | collective-permute-done | bytes 426016 | tf_op jit(solution)/shard_map/ppermute | solution.py:120
  129.2 6.4 %collective-permute-start.14 = (bf16[4,208,256]{2,1,0:T(8,128)(2,1)S(1)}, bf16[4,208,256]{2,1,0:T(8,128)(2,1)S(1)}, u32[]{:S(2)}, u32[]{:S(2)}) collective-permute-start(bf16[4,208,256]{2,1,0:T(8,128)(2,1)S(1)} %get-tuple-element.122), channel_id=1, source_target_pairs={{0,2},{1,3},{2,0},{3,1},{4,6},{5,7},{6,4},{7,5},{8,10},{9,11},{10,... | collective-permute-start | bytes 1277960 | tf_op jit(solution)/shard_map/ppermute | solution.py:120
  135.6 6.1 %collective-permute-done.14 = bf16[4,208,256]{2,1,0:T(8,128)(2,1)S(1)} collective-permute-done((bf16[4,208,256]{2,1,0:T(8,128)(2,1)S(1)}, bf16[4,208,256]{2,1,0:T(8,128)(2,1)S(1)}, u32[]{:S(2)}, u32[]{:S(2)}) %collective-permute-start.14) | collective-permute-done | bytes 426016 | tf_op jit(solution)/shard_map/ppermute | solution.py:120
  147.4 32.4 %middle.1 = (bf16[512,768]{1,0:T(8,128)(2,1)}, f32[512,768]{1,0:T(8,128)}, bf16[512,768]{1,0:T(8,128)(2,1)}, f32[512,128]{1,0:T(8,128)}, bf16[4,4,208,256]{3,2,1...) custom-call(bf16[512,768]{1,0:T(8,128)(2,1)} %bitcast.218, ...), custom_call_target="tpu_custom_call" | custom-call | flops 248000004096 | bytes 31000000 | tf_op jit(solution)/shard_map/middle/pallas_call | solution.py:813
  186.9 9.7 %back_query.2 = (bf16[256,768]{1,0:T(8,128)(2,1)}, f32[256,768]{1,0:T(8,128)}, bf16[2,12,128,128]{3,2,1,0:T(8,128)(2,1)}, f32[1,1]{1,0:T(1,128)}) custom-call(bf16[512,768]{1,0:T(8,128)(2,1)} %get-tuple-element.66.refs_0_, bf16[512,768]{1,0:T(8,128)(2,1)} %get-tuple-element.61.v_ref.refs_1_, bf16[512,3072]{1,0:T(8,128)(2,1)} %get-tuple-element.59.phq_ref.refs_2_, ...), custom_call_target="tpu_custom_call" | custom-call | flops 64000000000 | bytes 8000000 | tf_op jit(solution)/shard_map/back_query/pallas_call | solution.py:862
  198.6 11.6 %grads.1 = (bf16[16,24,3200]{2,1,0:T(8,128)(2,1)}, bf16[16,24,3200]{2,1,0:T(8,128)(2,1)}, bf16[16,120,768]{2,1,0:T(8,128)(2,1)}, bf16[16,120,768]{2,1,0:T(8,128)(2,1)}, f32[1,1]{1,0:T(1,128)}) custom-call(s32[1]{0:T(128)} %bitcast.63.core_ref, bf16[512,768]{1,0:T(8,128)(2,1)} %get-tuple-element.80.attn_ref, bf16[512,768]{1,0:T(8,128)(2,1)} %get-tuple-element.81.dao_ref, ...), custom_call_target="tpu_custom_call" | custom-call | flops 80000000000 | bytes 10000000 | tf_op jit(solution)/shard_map/grads/pallas_call | solution.py:1030
  217.0 9.7 %back_query.3 = (bf16[256,768]{1,0:T(8,128)(2,1)}, f32[256,768]{1,0:T(8,128)}, bf16[2,12,128,128]{3,2,1,0:T(8,128)(2,1)}, f32[1,1]{1,0:T(1,128)}) custom-call(bf16[512,768]{1,0:T(8,128)(2,1)} %get-tuple-element.66.refs_0_, bf16[512,768]{1,0:T(8,128)(2,1)} %get-tuple-element.61.v_ref.refs_1_, bf16[512,3072]{1,0:T(8,128)(2,1)} %get-tuple-element.59.phq_ref.refs_2_, ...), custom_call_target="tpu_custom_call" | custom-call | flops 64000000000 | bytes 8000000 | tf_op jit(solution)/shard_map/back_query/pallas_call | solution.py:862
  226.7 13.6 %collective-permute-done.19 = bf16[4,208,256]{2,1,0:T(8,128)(2,1)S(1)} collective-permute-done((bf16[4,208,256]{2,1,0:T(8,128)(2,1)S(1)}, bf16[4,208,256]{2,1,0:T(8,128)(2,1)S(1)}, u32[]{:S(2)}, u32[]{:S(2)}) %collective-permute-start.19) | collective-permute-done | bytes 426016 | tf_op jit(solution)/shard_map/ppermute | solution.py:120
  241.7 11.0 %collective-permute-done.20 = bf16[4,208,256]{2,1,0:T(8,128)(2,1)S(1)} collective-permute-done((bf16[4,208,256]{2,1,0:T(8,128)(2,1)S(1)}, bf16[4,208,256]{2,1,0:T(8,128)(2,1)S(1)}, u32[]{:S(2)}, u32[]{:S(2)}) %collective-permute-start.20) | collective-permute-done | bytes 426016 | tf_op jit(solution)/shard_map/ppermute | solution.py:120
  267.1 13.5 %back_key.1.dkv_ref = bf16[512,1536]{1,0:T(8,128)(2,1)} custom-call(bf16[512,768]{1,0:T(8,128)(2,1)} %get-tuple-element.72.k_ref, bf16[512,768]{1,0:T(8,128)(2,1)} %get-tuple-element.61.v_ref.refs_1_, bf16[512,3072]{1,0:T(8,128)(2,1)} %get-tuple-element.59.phq_ref.refs_2_, bf16[512,3072]{1,0:T(8,128)(2,1)} %get-tuple-element.60.phk_ref.refs_3_, ...), custom_call_target="tpu_custom_call" | custom-call | flops 103999995904 | bytes 13000000 | tf_op jit(solution)/shard_map/back_key/pallas_call | solution.py:896
  280.6 6.1 %first_grads.1 = (bf16[16,24,1280]{2,1,0:T(8,128)(2,1)}, bf16[16,24,1280]{2,1,0:T(8,128)(2,1)}, bf16[16,24,1152]{2,1,0:T(8,128)(2,1)}, bf16[16,24,1152]{2,1,0:T(8,128)(2,1)}) custom-call(s32[1]{0:T(128)} %bitcast.63.core_ref, bf16[512,768]{1,0:T(8,128)(2,1)} %bitcast.219, bf16[512,768]{1,0:T(8,128)(2,1)} %copy-done.26, bf16[512,1536]{1,0:T(8,128)(2,1)} %back_key.1.dkv_ref), custom_call_target="tpu_custom_call" | custom-call | flops 48000000000 | bytes 6000000 | tf_op jit(solution)/shard_map/first_grads/pallas_call | solution.py:1095
  287.2 4.6 %collective-permute-done.26 = bf16[2,2,2,1,1,24,3200]{6,5,4,3,2,1,0:T(8,128)(2,1)} collective-permute-done((bf16[2,2,2,1,1,24,3200]{6,5,4,3,2,1,0:T(8,128)(2,1)}, bf16[2,2,2,1,1,24,3200]{6,5,4,3,2,1,0:T(8,128)(2,1)}, u32[]{:S(2)}, u32[]{:S(2)}) %collective-permute-start.26) | collective-permute-done | bytes 1228832 | tf_op jit(solution)/shard_map/ppermute | solution.py:19
  306.8 5.6 %collective-permute-done.39 = bf16[1,2,2,1,1,24,3200]{6,5,4,3,2,1,0:T(8,128)(2,1)S(1)} collective-permute-done((bf16[1,2,2,1,1,24,3200]{6,5,4,3,2,1,0:T(8,128)(2,1)S(1)}, bf16[1,2,2,1,1,24,3200]{6,5,4,3,2,1,0:T(8,128)(2,1)S(1)}, u32[]{:S(2)}, u32[]{:S(2)}) %collective-permute-start.39) | collective-permute-done | bytes 614432 | tf_op jit(solution)/shard_map/ppermute | solution.py:19
  312.7 6.6 %input_grad.1 = (bf16[512,768]{1,0:T(8,128)(2,1)}, f32[1,1]{1,0:T(1,128)}) custom-call(bf16[512,768]{1,0:T(8,128)(2,1)} %copy-done.26, bf16[512,1536]{1,0:T(8,128)(2,1)} %back_key.1.dkv_ref, bf16[768,1280]{1,0:T(8,128)(2,1)} %get-tuple-element.93.wa_ref, bf16[768,1152]{1,0:T(8,128)(2,1)} %get-tuple-element.94.wb_ref, f32[512,768]{1,0:T(8,128)} %get-tuple-element.95.dr1_ref, ...), custom_call_target="tpu_custom_call" | custom-call | flops 48000000000 | bytes 6000000 | tf_op jit(solution)/shard_map/input_grad/pallas_call | solution.py:1126
  320.1 7.2 %collective-permute-done.32 = bf16[2,2,2,1,1,24,1152]{6,5,4,3,2,1,0:T(8,128)(2,1)S(1)} collective-permute-done((bf16[2,2,2,1,1,24,1152]{6,5,4,3,2,1,0:T(8,128)(2,1)S(1)}, bf16[2,2,2,1,1,24,1152]{6,5,4,3,2,1,0:T(8,128)(2,1)S(1)}, u32[]{:S(2)}, u32[]{:S(2)}) %collective-permute-start.32) | collective-permute-done | bytes 442400 | tf_op jit(solution)/shard_map/ppermute | solution.py:19
  334.4 4.9 %collective-permute-done.34 = bf16[1,2,1,1,1,24,1152]{6,5,4,3,2,1,0:T(8,128)(2,1)S(1)} collective-permute-done((bf16[1,2,1,1,1,24,1152]{6,5,4,3,2,1,0:T(8,128)(2,1)S(1)}, bf16[1,2,1,1,1,24,1152]{6,5,4,3,2,1,0:T(8,128)(2,1)S(1)}, u32[]{:S(2)}, u32[]{:S(2)}) %collective-permute-start.34) | collective-permute-done | bytes 110624 | tf_op jit(solution)/shard_map/ppermute | solution.py:19
  346.8 4.7 %collective-permute-done.30 = bf16[1,2,1,1,1,24,1280]{6,5,4,3,2,1,0:T(8,128)(2,1)S(1)} collective-permute-done((bf16[1,2,1,1,1,24,1280]{6,5,4,3,2,1,0:T(8,128)(2,1)S(1)}, bf16[1,2,1,1,1,24,1280]{6,5,4,3,2,1,0:T(8,128)(2,1)S(1)}, u32[]{:S(2)}, u32[]{:S(2)}) %collective-permute-start.30) | collective-permute-done | bytes 122912 | tf_op jit(solution)/shard_map/ppermute | solution.py:19
  359.1 4.4 %collective-permute-done.38 = bf16[1,1,1,1,1,120,768]{6,5,4,3,2,1,0:T(8,128)(2,1)S(1)} collective-permute-done((bf16[1,1,1,1,1,120,768]{6,5,4,3,2,1,0:T(8,128)(2,1)S(1)}, bf16[1,1,1,1,1,120,768]{6,5,4,3,2,1,0:T(8,128)(2,1)S(1)}, u32[]{:S(2)}, u32[]{:S(2)}) %collective-permute-start.38) | collective-permute-done | bytes 184352 | tf_op jit(solution)/shard_map/ppermute | solution.py:19
  (292 shorter events, 124.4 us)
Async XLA Ops:
  7.3 140.1 %all-gather.2.cloned.1.call-start = ((), (), s32[]{:S(2)}) async-start(), calls=%async_computation | async-start | bytes 11151360 | tf_op jit(solution)/shard_map/all_gather | solution.py:1203
  9.8 10.8 %collective-permute-start = (bf16[1,24,1280]{2,1,0:T(8,128)(2,1)S(1)}, bf16[1,24,1280]{2,1,0:T(8,128)(2,1)S(1)}, u32[]{:S(2)}, u32[]{:S(2)}) collective-permute-start(bf16[1,24,1280]{2,1,0:T(8,128)(2,1)S(1)} %maximum_bitcast_fusion), channel_id=1, source_target_pairs={{0,8},{1,9},{2,10},{3,11},{4,12},{5,13},{6,14},{7,15},{8,0},{9,1},... | collective-permute-start | bytes 184328 | tf_op jit(solution)/shard_map/ppermute | solution.py:19
  33.5 13.8 %collective-permute-start.3 = (bf16[8,24,1280]{2,1,0:T(8,128)(2,1)S(1)}, bf16[8,24,1280]{2,1,0:T(8,128)(2,1)S(1)}, u32[]{:S(2)}, u32[]{:S(2)}) collective-permute-start(bf16[8,24,1280]{2,1,0:T(8,128)(2,1)S(1)} %pad_maximum_fusion.3), channel_id=1, source_target_pairs={{0,16},{1,17},{2,18},{3,19},{4,20},{5,21},{6,22},{7,23},{8,24},{9,... | collective-permute-start | bytes 1474568 | tf_op jit(solution)/shard_map/ppermute | solution.py:19
  35.1 13.8 %collective-permute-start.8 = (bf16[8,24,1152]{2,1,0:T(8,128)(2,1)S(1)}, bf16[8,24,1152]{2,1,0:T(8,128)(2,1)S(1)}, u32[]{:S(2)}, u32[]{:S(2)}) collective-permute-start(bf16[8,24,1152]{2,1,0:T(8,128)(2,1)S(1)} %pad_maximum_fusion.4), channel_id=1, source_target_pairs={{0,2},{1,3},{2,0},{3,1},{4,6},{5,7},{6,4},{7,5},{8,10},{9,11},{10,... | collective-permute-start | bytes 1327112 | tf_op jit(solution)/shard_map/ppermute | solution.py:19
  71.5 15.5 %collective-permute-start.11 = (bf16[4,208,256]{2,1,0:T(8,128)(2,1)S(1)}, bf16[4,208,256]{2,1,0:T(8,128)(2,1)S(1)}, u32[]{:S(2)}, u32[]{:S(2)}) collective-permute-start(bf16[4,208,256]{2,1,0:T(8,128)(2,1)S(1)} %fusion.20), channel_id=1, source_target_pairs={{0,2},{1,3},{2,0},{3,1},{4,6},{5,7},{6,4},{7,5},{8,10},{9,11},{10,... | collective-permute-start | bytes 1277960 | tf_op jit(solution)/shard_map/ppermute | solution.py:120
  87.8 21.5 %collective-permute-start.12 = (bf16[4,208,256]{2,1,0:T(8,128)(2,1)S(1)}, bf16[4,208,256]{2,1,0:T(8,128)(2,1)S(1)}, u32[]{:S(2)}, u32[]{:S(2)}) collective-permute-start(bf16[4,208,256]{2,1,0:T(8,128)(2,1)S(1)} %fusion.25), channel_id=1, source_target_pairs={{0,4},{1,5},{2,6},{3,7},{4,8},{5,9},{6,10},{7,11},{8,12},{9,13},{1... | collective-permute-start | bytes 1277960 | tf_op jit(solution)/shard_map/ppermute | solution.py:120
  110.3 18.5 %collective-permute-start.13 = (bf16[4,208,256]{2,1,0:T(8,128)(2,1)S(1)}, bf16[4,208,256]{2,1,0:T(8,128)(2,1)S(1)}, u32[]{:S(2)}, u32[]{:S(2)}) collective-permute-start(bf16[4,208,256]{2,1,0:T(8,128)(2,1)S(1)} %fusion.12), channel_id=1, source_target_pairs={{0,8},{1,9},{2,10},{3,11},{4,12},{5,13},{6,14},{7,15},{16,24},{17,... | collective-permute-start | bytes 1277960 | tf_op jit(solution)/shard_map/ppermute | solution.py:120
  129.2 12.5 %collective-permute-start.14 = (bf16[4,208,256]{2,1,0:T(8,128)(2,1)S(1)}, bf16[4,208,256]{2,1,0:T(8,128)(2,1)S(1)}, u32[]{:S(2)}, u32[]{:S(2)}) collective-permute-start(bf16[4,208,256]{2,1,0:T(8,128)(2,1)S(1)} %get-tuple-element.122), channel_id=1, source_target_pairs={{0,2},{1,3},{2,0},{3,1},{4,6},{5,7},{6,4},{7,5},{8,10},{9,11},{10,... | collective-permute-start | bytes 1277960 | tf_op jit(solution)/shard_map/ppermute | solution.py:120
  184.8 12.2 %collective-permute-start.17 = (bf16[4,208,256]{2,1,0:T(8,128)(2,1)S(1)}, bf16[4,208,256]{2,1,0:T(8,128)(2,1)S(1)}, u32[]{:S(2)}, u32[]{:S(2)}) collective-permute-start(bf16[4,208,256]{2,1,0:T(8,128)(2,1)S(1)} %fusion.22.tie_ref), channel_id=1, source_target_pairs={{15,13},{14,12},{13,15},{12,14},{11,9},{10,8},{9,11},{8,10},{7,5},... | collective-permute-start | bytes 1277960 | tf_op jit(solution)/shard_map/ppermute | solution.py:120
  197.3 17.1 %collective-permute-start.18 = (bf16[4,208,256]{2,1,0:T(8,128)(2,1)S(1)}, bf16[4,208,256]{2,1,0:T(8,128)(2,1)S(1)}, u32[]{:S(2)}, u32[]{:S(2)}) collective-permute-start(bf16[4,208,256]{2,1,0:T(8,128)(2,1)S(1)} %fusion.24), channel_id=1, source_target_pairs={{15,11},{14,10},{13,9},{12,8},{11,7},{10,6},{9,5},{8,4},{7,3},{6,2... | collective-permute-start | bytes 1277960 | tf_op jit(solution)/shard_map/ppermute | solution.py:120
  210.2 46.7 %collective-permute-start.22 = (bf16[16,120,768]{2,1,0:T(8,128)(2,1)}, bf16[16,120,768]{2,1,0:T(8,128)(2,1)}, u32[]{:S(2)}, u32[]{:S(2)}) collective-permute-start(bf16[16,120,768]{2,1,0:T(8,128)(2,1)} %get-tuple-element.91), channel_id=1, source_target_pairs={{0,1},{1,0},{2,3},{3,2},{4,5},{5,4},{6,7},{7,6},{8,9},{9,8},{10,11... | collective-permute-start | bytes 8847368 | tf_op jit(solution)/shard_map/ppermute | solution.py:19
  210.2 43.0 %collective-permute-start.21 = (bf16[16,24,3200]{2,1,0:T(8,128)(2,1)}, bf16[16,24,3200]{2,1,0:T(8,128)(2,1)}, u32[]{:S(2)}, u32[]{:S(2)}) collective-permute-start(bf16[16,24,3200]{2,1,0:T(8,128)(2,1)} %get-tuple-element.89), channel_id=1, source_target_pairs={{0,1},{1,0},{2,3},{3,2},{4,5},{5,4},{6,7},{7,6},{8,9},{9,8},{10,11... | collective-permute-start | bytes 7372808 | tf_op jit(solution)/shard_map/ppermute | solution.py:19
  215.4 24.9 %collective-permute-start.19 = (bf16[4,208,256]{2,1,0:T(8,128)(2,1)S(1)}, bf16[4,208,256]{2,1,0:T(8,128)(2,1)S(1)}, u32[]{:S(2)}, u32[]{:S(2)}) collective-permute-start(bf16[4,208,256]{2,1,0:T(8,128)(2,1)S(1)} %fusion.17), channel_id=1, source_target_pairs={{15,7},{14,6},{13,5},{12,4},{11,3},{10,2},{9,1},{8,0},{31,23},{30,... | collective-permute-start | bytes 1277960 | tf_op jit(solution)/shard_map/ppermute | solution.py:120
  241.4 11.3 %collective-permute-start.20 = (bf16[4,208,256]{2,1,0:T(8,128)(2,1)S(1)}, bf16[4,208,256]{2,1,0:T(8,128)(2,1)S(1)}, u32[]{:S(2)}, u32[]{:S(2)}) collective-permute-start(bf16[4,208,256]{2,1,0:T(8,128)(2,1)S(1)} %get-tuple-element.120), channel_id=1, source_target_pairs={{15,13},{14,12},{13,15},{12,14},{11,9},{10,8},{9,11},{8,10},{7,5},... | collective-permute-start | bytes 1277960 | tf_op jit(solution)/shard_map/ppermute | solution.py:120
  262.2 29.6 %collective-permute-start.26 = (bf16[2,2,2,1,1,24,3200]{6,5,4,3,2,1,0:T(8,128)(2,1)}, bf16[2,2,2,1,1,24,3200]{6,5,4,3,2,1,0:T(8,128)(2,1)}, u32[]{:S(2)}, u32[]{:S(2)}) collective-permute-start(bf16[2,2,2,1,1,24,3200]{6,5,4,3,2,1,0:T(8,128)(2,1)} %constant_dynamic-slice_fusion.15), channel_id=1, source_target_pairs={{0,2},{1,3},{2,0},{3,1},{4,6},{5,7},{6,4},{7,5},{8,10},{9,11},{10,... | collective-permute-start | bytes 3686408 | tf_op jit(solution)/shard_map/ppermute | solution.py:19
  263.8 35.5 %collective-permute-start.27 = (bf16[1,2,2,2,1,120,768]{6,5,4,3,2,1,0:T(8,128)(2,1)}, bf16[1,2,2,2,1,120,768]{6,5,4,3,2,1,0:T(8,128)(2,1)}, u32[]{:S(2)}, u32[]{:S(2)}) collective-permute-start(bf16[1,2,2,2,1,120,768]{6,5,4,3,2,1,0:T(8,128)(2,1)} %constant_dynamic-slice_fusion.14), channel_id=1, source_target_pairs={{0,16},{1,17},{2,18},{3,19},{4,20},{5,21},{6,22},{7,23},{8,24},{9,... | collective-permute-start | bytes 4423688 | tf_op jit(solution)/shard_map/ppermute | solution.py:19
  286.7 16.2 %collective-permute-start.25 = (bf16[16,24,1152]{2,1,0:T(8,128)(2,1)}, bf16[16,24,1152]{2,1,0:T(8,128)(2,1)S(1)}, u32[]{:S(2)}, u32[]{:S(2)}) collective-permute-start(bf16[16,24,1152]{2,1,0:T(8,128)(2,1)} %get-tuple-element.99), channel_id=1, source_target_pairs={{0,1},{1,0},{2,3},{3,2},{4,5},{5,4},{6,7},{7,6},{8,9},{9,8},{10,11... | collective-permute-start | bytes 2654216 | tf_op jit(solution)/shard_map/ppermute | solution.py:19
  286.7 18.1 %collective-permute-start.24 = (bf16[16,24,1280]{2,1,0:T(8,128)(2,1)}, bf16[16,24,1280]{2,1,0:T(8,128)(2,1)S(1)}, u32[]{:S(2)}, u32[]{:S(2)}) collective-permute-start(bf16[16,24,1280]{2,1,0:T(8,128)(2,1)} %get-tuple-element.97), channel_id=1, source_target_pairs={{0,1},{1,0},{2,3},{3,2},{4,5},{5,4},{6,7},{7,6},{8,9},{9,8},{10,11... | collective-permute-start | bytes 2949128 | tf_op jit(solution)/shard_map/ppermute | solution.py:19
  293.4 19.0 %collective-permute-start.39 = (bf16[1,2,2,1,1,24,3200]{6,5,4,3,2,1,0:T(8,128)(2,1)S(1)}, bf16[1,2,2,1,1,24,3200]{6,5,4,3,2,1,0:T(8,128)(2,1)S(1)}, u32[]{:S(2)}, u32[]{:S(2)}) collective-permute-start(bf16[1,2,2,1,1,24,3200]{6,5,4,3,2,1,0:T(8,128)(2,1)S(1)} %constant_dynamic-slice_fusion.2), channel_id=1, source_target_pairs={{0,16},{1,17},{2,18},{3,19},{4,20},{5,21},{6,22},{7,23},{8,24},{9,... | collective-permute-start | bytes 1843208 | tf_op jit(solution)/shard_map/ppermute | solution.py:19
  301.1 27.9 %collective-permute-start.36 = (bf16[1,2,2,1,1,120,768]{6,5,4,3,2,1,0:T(8,128)(2,1)S(1)}, bf16[1,2,2,1,1,120,768]{6,5,4,3,2,1,0:T(8,128)(2,1)S(1)}, u32[]{:S(2)}, u32[]{:S(2)}) collective-permute-start(bf16[1,2,2,1,1,120,768]{6,5,4,3,2,1,0:T(8,128)(2,1)S(1)} %constant_dynamic-slice_fusion.5), channel_id=1, source_target_pairs={{0,2},{1,3},{2,0},{3,1},{4,6},{5,7},{6,4},{7,5},{8,10},{9,11},{10,... | collective-permute-start | bytes 2211848 | tf_op jit(solution)/shard_map/ppermute | solution.py:19
  303.1 24.1 %collective-permute-start.32 = (bf16[2,2,2,1,1,24,1152]{6,5,4,3,2,1,0:T(8,128)(2,1)S(1)}, bf16[2,2,2,1,1,24,1152]{6,5,4,3,2,1,0:T(8,128)(2,1)S(1)}, u32[]{:S(2)}, u32[]{:S(2)}) collective-permute-start(bf16[2,2,2,1,1,24,1152]{6,5,4,3,2,1,0:T(8,128)(2,1)S(1)} %constant_dynamic-slice_fusion.9), channel_id=1, source_target_pairs={{0,2},{1,3},{2,0},{3,1},{4,6},{5,7},{6,4},{7,5},{8,10},{9,11},{10,... | collective-permute-start | bytes 1327112 | tf_op jit(solution)/shard_map/ppermute | solution.py:19
  305.1 28.4 %collective-permute-start.28 = (bf16[1,2,2,2,1,24,1280]{6,5,4,3,2,1,0:T(8,128)(2,1)S(1)}, bf16[1,2,2,2,1,24,1280]{6,5,4,3,2,1,0:T(8,128)(2,1)S(1)}, u32[]{:S(2)}, u32[]{:S(2)}) collective-permute-start(bf16[1,2,2,2,1,24,1280]{6,5,4,3,2,1,0:T(8,128)(2,1)S(1)} %constant_dynamic-slice_fusion.13), channel_id=1, source_target_pairs={{0,16},{1,17},{2,18},{3,19},{4,20},{5,21},{6,22},{7,23},{8,24},{9,... | collective-permute-start | bytes 1474568 | tf_op jit(solution)/shard_map/ppermute | solution.py:19
  320.0 9.4 %collective-permute-start.41 = (bf16[1,1,1,1,1,24,3200]{6,5,4,3,2,1,0:T(8,128)(2,1)S(1)}, bf16[1,1,1,1,1,24,3200]{6,5,4,3,2,1,0:T(8,128)(2,1)S(1)}, u32[]{:S(2)}, u32[]{:S(2)}) collective-permute-start(bf16[1,1,1,1,1,24,3200]{6,5,4,3,2,1,0:T(8,128)(2,1)S(1)} %constant_dynamic-slice_fusion), channel_id=1, source_target_pairs={{0,8},{1,9},{2,10},{3,11},{4,12},{5,13},{6,14},{7,15},{8,0},{9,1},... | collective-permute-start | bytes 460808 | tf_op jit(solution)/shard_map/ppermute | solution.py:19
  329.3 17.4 %collective-permute-start.37 = (bf16[1,2,1,1,1,120,768]{6,5,4,3,2,1,0:T(8,128)(2,1)S(1)}, bf16[1,2,1,1,1,120,768]{6,5,4,3,2,1,0:T(8,128)(2,1)S(1)}, u32[]{:S(2)}, u32[]{:S(2)}) collective-permute-start(bf16[1,2,1,1,1,120,768]{6,5,4,3,2,1,0:T(8,128)(2,1)S(1)} %constant_dynamic-slice_fusion.4), channel_id=1, source_target_pairs={{0,4},{1,5},{2,6},{3,7},{4,0},{5,1},{6,2},{7,3},{8,12},{9,13},{10,... | collective-permute-start | bytes 1105928 | tf_op jit(solution)/shard_map/ppermute | solution.py:19
  (62 other events, 557.9 us)
Sparse Core Ops, SparseCore 0:
  24.0 95.9 all-gather.1
where the time goes:
time: 379 us; the launch traced here: 372 us
  waiting for transfers between devices  132 us (35%)
  Pallas kernels  112 us (30%)
  starting transfers between devices  61 us (16%)
  local copies, waits for them, and re-layouts  27 us (7%)
  other arithmetic  24.5 us (6%)
  between operations  15.6 us (4%)
    ppermute x12, waiting for transfers between devices, seq_perm(): return lax.ppermute(value, 'seq', pairs)  67.6 us
    ppermute x30, waiting for transfers between devices, flat_xor(): return lax.ppermute(value, AXES, [(i, i ^ mask) for i in range(n)])  64.2 us
    pallas_call x1, Pallas kernels, call_middle(): pl.pallas_call(partial(middle_kernel, block, heads, d, 768, tiled, shard_...  32.4 us
    ppermute x30, starting transfers between devices, flat_xor(): return lax.ppermute(value, AXES, [(i, i ^ mask) for i in range(n)])  30.9 us
    ppermute x12, starting transfers between devices, seq_perm(): return lax.ppermute(value, 'seq', pairs)  30.1 us
    pallas_call x2, Pallas kernels, call_back_query(): pl.pallas_call(kernel, grid=(1,), in_specs=[rs(width), rs(width), rs(phq....  19.4 us
    pallas_call x1, Pallas kernels, call_back_key(): pl.pallas_call(kernel, grid=(steps,), in_specs=[row_spec(n, width), row_s...  13.5 us
    pallas_call x1, Pallas kernels, call_features_tiled(): pl.pallas_call(partial(features_tiled_kernel, block, heads, d, (a.order,...  12.5 us
  transfers between devices with their start and end apart: 43, of which 27 were waited for; matrix products, arithmetic and copies ran while one was open for 11% of the time, Pallas kernels for 21%

commit v1 on v0

--- a/solution.py
+++ b/solution.py
@@ -291,7 +291,7 @@
 
 def features_tiled_kernel(
     block, heads, d, orders, shard_rows, me_ref, x_ref, own_a, oth_a, own_b, oth_b, proj_ref, tg_ref,
-    q_ref, k_ref, v_ref, phq_ref, phk_ref, tail_ref, wa_ref, wb_ref, z_scr, bias,
+    k_ref, v_ref, phk_ref, tail_ref, wa_ref, wb_ref, bias, z_scr,
 ):
     @pl.when(pl.program_id(0) == 0)
     def _():
@@ -304,16 +304,25 @@
                 )
             )
 
-    features_kernel(
-        block, heads, d, x_ref, wa_ref, wb_ref, bias, proj_ref, tg_ref,
-        q_ref, k_ref, v_ref, phq_ref, phk_ref, tail_ref, z_scr,
-    )
+    parts = ((1, (k_ref, phk_ref)), (2, (v_ref, None)))
+    project_parts(block, heads, d, parts, x_ref, wa_ref, wb_ref, bias, proj_ref)
+    tail_parts(block, heads, d, tg_ref, v_ref, phk_ref, tail_ref, z_scr)
 
 
 def features_kernel(
     block, heads, d, x_ref, wa_ref, wb_ref, b_ref, proj_ref, tg_ref,
     q_ref, k_ref, v_ref, phq_ref, phk_ref, tail_ref, z_scr,
 ):
+    parts = ((1, (k_ref, phk_ref)), (2, (v_ref, None)), (0, (q_ref, phq_ref)))
+    project_parts(block, heads, d, parts, x_ref, wa_ref, wb_ref, b_ref, proj_ref)
+    tail_parts(block, heads, d, tg_ref, v_ref, phk_ref, tail_ref, z_scr)
+
+
+def query_kernel(block, heads, d, x_ref, wa_ref, b_ref, proj_ref, q_ref, phq_ref):
+    project_parts(block, heads, d, ((0, (q_ref, phq_ref)),), x_ref, wa_ref, None, b_ref, proj_ref)
+
+
+def project_parts(block, heads, d, parts, x_ref, wa_ref, wb_ref, b_ref, proj_ref):
     width = heads * d
     m = proj_ref.shape[2]
     pair = 2 * d
@@ -323,7 +332,7 @@
     rows = x.shape[0]
     low = lane_low((rows, pair), d)
     chunk = width // 2
-    for t, (z_ref, ph_ref) in ((1, (k_ref, phk_ref)), (2, (v_ref, None)), (0, (q_ref, phq_ref))):
+    for t, (z_ref, ph_ref) in parts:
         for i in range(2):
             col = t * width + i * chunk
             w = wa_ref[:, col : col + chunk] if col < 3 * chunk else wb_ref[:, col - 3 * chunk : col - 2 * chunk]
@@ -340,8 +349,13 @@
                     h = 2 * (i * (chunk // pair) + p) + e
                     u = mm(zp, proj_ref[h])
                     ph_ref[:, h * m : (h + 1) * m] = (jnp.exp(u - 0.5 * sums[e]) * root).astype(bf16)
+
+
+def tail_parts(block, heads, d, tg_ref, v_ref, phk_ref, tail_ref, z_scr):
+    m = phk_ref.shape[1] // heads
+    pair = 2 * d
     per = heads // 4
-    for s in range(rows // block):
+    for s in range(v_ref.shape[0] // block):
         r = slice(s * block, (s + 1) * block)
         tg = tg_ref[r, :].astype(bf16)
         for p in range(heads // 2):
@@ -770,16 +784,34 @@
         in_specs=[pl.BlockSpec(memory_space=pltpu.SMEM), row_spec(n, width)]
         + [whole_spec(t.shape) for t in parts]
         + [whole_spec(proj.shape), row_spec(n, 1)],
-        out_specs=[row_spec(n, width)] * 3
-        + [row_spec(n, heads * m)] * 2
-        + [lead_spec(st), whole_spec(wa), whole_spec(wb)],
-        out_shape=[sds((rows, width), bf16)] * 3
-        + [sds((rows, heads * m), bf16)] * 2
-        + [sds((rows // block,) + st[1:], bf16), sds(wa, bf16), sds(wb, bf16)],
-        scratch_shapes=[pltpu.VMEM((16, m), f32), pltpu.VMEM((8, 3 * width), f32)],
+        out_specs=[row_spec(n, width)] * 2
+        + [row_spec(n, heads * m), lead_spec(st)]
+        + [whole_spec(t) for t in (wa, wb, (8, 3 * width))],
+        out_shape=[sds((rows, width), bf16)] * 2
+        + [sds((rows, heads * m), bf16), sds((rows // block,) + st[1:], bf16)]
+        + [sds(wa, bf16), sds(wb, bf16), sds((8, 3 * width), f32)],
+        scratch_shapes=[pltpu.VMEM((16, m), f32)],
         name="features",
-        **params(12),
+        **params(9),
     )(my_flat().astype(jnp.int32).reshape(1), x, *parts, proj, tg)
+
+
+def call_query(x, wa, bias, proj, block, heads, d):
+    rows, width = x.shape
+    m = proj.shape[2]
+    n = STEP_SEQS * block
+    return pl.pallas_call(
+        partial(query_kernel, block, heads, d),
+        grid=(rows // n,),
+        in_specs=[
+            row_spec(n, width), pl.BlockSpec((width, width), lambda i: (0, 0)),
+            whole_spec(bias.shape), whole_spec(proj.shape),
+        ],
+        out_specs=[row_spec(n, width), row_spec(n, heads * m)],
+        out_shape=[sds((rows, width), bf16), sds((rows, heads * m), bf16)],
+        name="query",
+        **params(4),
+    )(x, wa, bias, proj)
 
 
 def call_local(phq, phk, v, gates, id_rows, block, heads, d):
@@ -1206,9 +1238,10 @@
         index = slot(gather_a.order, my_flat(), device) + ((device ^ my_flat()) & 1) * (n_dev // 2)
         chosen = (index[:, None] == jnp.arange(n_dev)[None, :]).astype(f32)
         last_all = jnp.sum(chosen[:, :, None] * ids.astype(f32)[None], axis=1)
-        q, k, v, phq, phk, tails, w_a, w_b = call_features_tiled(
+        k, v, phk, tails, w_a, w_b, bias = call_features_tiled(
             x, gather_a, gather_b, proj, tail_gate.reshape(rows, 1), shard_rows, *dims
         )
+        q, phq = call_query(x, w_a, bias, proj, *dims)
     else:
         flat = jnp.concatenate(vectors + (ids_b,))
         flat = jnp.pad(flat, (0, -flat.shape[0] % 128)).reshape(-1, 128)

time: 379 us -> 400 us (1.055)
  waiting for transfers between devices: 132 us -> 161 us
  starting transfers between devices: 61 us -> 47.3 us
    ppermute x12, waiting for transfers between devices: 67.6 us -> 97.4 us  [seq_perm(): return lax.ppermute(value, 'seq', pairs)]
    ppermute x12, starting transfers between devices: 30.1 us -> 18.1 us  [seq_perm(): return lax.ppermute(value, 'seq', pairs)]
    pallas_call x0 -> x1, Pallas kernels: none -> 5.64 us  [call_query(): pl.pallas_call(partial(query_kernel, block, heads, d), grid=(rows // n,),...]
  transfers between devices with their start and end apart: 43 -> 43, of which waited for: 27 -> 25; matrix products, arithmetic and copies ran while one was open for 11% -> 11% of each run, Pallas kernels for 21% -> 21%
where the time goes in v1:
time: 400 us; the launch traced here: 393 us
  waiting for transfers between devices  161 us (40%)
  Pallas kernels  114 us (28%)
  starting transfers between devices  47.3 us (12%)
  local copies, waits for them, and re-layouts  29.8 us (7%)
  other arithmetic  24.6 us (6%)
  between operations  15.4 us (4%)
    ppermute x12, waiting for transfers between devices, seq_perm(): return lax.ppermute(value, 'seq', pairs)  97.4 us
    ppermute x30, waiting for transfers between devices, flat_xor(): return lax.ppermute(value, AXES, [(i, i ^ mask) for i in range(n)])  63.9 us
    pallas_call x1, Pallas kernels, call_middle(): pl.pallas_call(partial(middle_kernel, block, heads, d, 768, tiled, shard_...  32.4 us
    ppermute x30, starting transfers between devices, flat_xor(): return lax.ppermute(value, AXES, [(i, i ^ mask) for i in range(n)])  29.2 us
    pallas_call x2, Pallas kernels, call_back_query(): pl.pallas_call(kernel, grid=(1,), in_specs=[rs(width), rs(width), rs(phq....  19.4 us
    ppermute x12, starting transfers between devices, seq_perm(): return lax.ppermute(value, 'seq', pairs)  18.1 us
    pallas_call x1, Pallas kernels, call_back_key(): pl.pallas_call(kernel, grid=(steps,), in_specs=[row_spec(n, width), row_s...  13.5 us
    pallas_call x1, Pallas kernels, call_grads(): pl.pallas_call(partial(grads_kernel, shard_rows), grid=(steps,), in_specs...  11.6 us
  transfers between devices with their start and end apart: 43, of which 25 were waited for; matrix products, arithmetic and copies ran while one was open for 11% of the time, Pallas kernels for 21%

profile of v1, /device:TPU:0, one launch (start us, length us, event | category | flops | bytes accessed | tf_op | source)
XLA Modules:
  0.0 392.9 jit_solution(9270225959657566183)
XLA Ops:
  37.5 8.2 %collective-permute-done.3 = bf16[8,24,1280]{2,1,0:T(8,128)(2,1)S(1)} collective-permute-done((bf16[8,24,1280]{2,1,0:T(8,128)(2,1)S(1)}, bf16[8,24,1280]{2,1,0:T(8,128)(2,1)S(1)}, u32[]{:S(2)}, u32[]{:S(2)}) %collective-permute-start.3) | collective-permute-done | bytes 491552 | tf_op jit(solution)/shard_map/ppermute | solution.py:19
  54.1 9.1 %features.1 = (bf16[512,768]{1,0:T(8,128)(2,1)}, bf16[512,768]{1,0:T(8,128)(2,1)}, bf16[512,3072]{1,0:T(8,128)(2,1)}, bf16[4,4,208,256]{3,2,1,0:T(8,128)(2,1)}, ...) custom-call(s32[1]{0:T(128)} %bitcast.2.me_ref, bf16[512,768]{1,0:T(8,128)(2,1)} %bitcast.218, ...), custom_call_target="tpu_custom_call" | custom-call | flops 71999995904 | bytes 9000000 | tf_op jit(solution)/shard_map/features/pallas_call | solution.py:781
  65.5 5.6 %query.1 = (bf16[512,768]{1,0:T(8,128)(2,1)}, bf16[512,3072]{1,0:T(8,128)(2,1)}) custom-call(bf16[512,768]{1,0:T(8,128)(2,1)} %bitcast.219, bf16[768,1280]{1,0:T(8,128)(2,1)} %get-tuple-element.60.wa_ref, f32[8,2304]{1,0:T(8,128)} %get-tuple-element.61.b_ref, bf16[12,128,256]{2,1,0:T(8,128)(2,1)} %bitcast.196), custom_call_target="tpu_custom_call" | custom-call | flops 32000000000 | bytes 4000000 | tf_op jit(solution)/shard_map/query/pallas_call | solution.py:803
  74.2 8.3 %local.1 = (bf16[4,12,128,128]{3,2,1,0:T(8,128)(2,1)}, f32[512,1536]{1,0:T(8,128)}, f32[1,1]{1,0:T(1,128)}) custom-call(bf16[512,3072]{1,0:T(8,128)(2,1)} %get-tuple-element.62.phq_ref.refs_2_, bf16[512,3072]{1,0:T(8,128)(2,1)} %get-tuple-element.63.phk_ref.refs_3_, bf16[512,768]{1,0:T(8,128)(2,1)} %get-tuple-element.64.v_ref.refs_1_, ...), custom_call_target="tpu_custom_call" | custom-call | flops 64000000000 | bytes 8000000 | tf_op jit(solution)/shard_map/local/pallas_call | solution.py:820
  82.6 8.6 %collective-permute-done.11 = bf16[4,208,256]{2,1,0:T(8,128)(2,1)S(1)} collective-permute-done((bf16[4,208,256]{2,1,0:T(8,128)(2,1)S(1)}, bf16[4,208,256]{2,1,0:T(8,128)(2,1)S(1)}, u32[]{:S(2)}, u32[]{:S(2)}) %collective-permute-start.11) | collective-permute-done | bytes 426016 | tf_op jit(solution)/shard_map/ppermute | solution.py:120
  95.2 13.5 %collective-permute-done.12 = bf16[4,208,256]{2,1,0:T(8,128)(2,1)S(1)} collective-permute-done((bf16[4,208,256]{2,1,0:T(8,128)(2,1)S(1)}, bf16[4,208,256]{2,1,0:T(8,128)(2,1)S(1)}, u32[]{:S(2)}, u32[]{:S(2)}) %collective-permute-start.12) | collective-permute-done | bytes 426016 | tf_op jit(solution)/shard_map/ppermute | solution.py:120
  109.7 5.7 %collective-permute-start.13 = (bf16[4,208,256]{2,1,0:T(8,128)(2,1)S(1)}, bf16[4,208,256]{2,1,0:T(8,128)(2,1)S(1)}, u32[]{:S(2)}, u32[]{:S(2)}) collective-permute-start(bf16[4,208,256]{2,1,0:T(8,128)(2,1)S(1)} %fusion.12), channel_id=1, source_target_pairs={{0,8},{1,9},{2,10},{3,11},{4,12},{5,13},{6,14},{7,15},{16,24},{17,... | collective-permute-start | bytes 1277960 | tf_op jit(solution)/shard_map/ppermute | solution.py:120
  115.5 18.1 %collective-permute-done.13 = bf16[4,208,256]{2,1,0:T(8,128)(2,1)S(1)} collective-permute-done((bf16[4,208,256]{2,1,0:T(8,128)(2,1)S(1)}, bf16[4,208,256]{2,1,0:T(8,128)(2,1)S(1)}, u32[]{:S(2)}, u32[]{:S(2)}) %collective-permute-start.13) | collective-permute-done | bytes 426016 | tf_op jit(solution)/shard_map/ppermute | solution.py:120
  134.8 9.0 %collective-permute-done.14 = bf16[4,208,256]{2,1,0:T(8,128)(2,1)S(1)} collective-permute-done((bf16[4,208,256]{2,1,0:T(8,128)(2,1)S(1)}, bf16[4,208,256]{2,1,0:T(8,128)(2,1)S(1)}, u32[]{:S(2)}, u32[]{:S(2)}) %collective-permute-start.14) | collective-permute-done | bytes 426016 | tf_op jit(solution)/shard_map/ppermute | solution.py:120
  149.9 32.4 %middle.1 = (bf16[512,768]{1,0:T(8,128)(2,1)}, f32[512,768]{1,0:T(8,128)}, bf16[512,768]{1,0:T(8,128)(2,1)}, f32[512,128]{1,0:T(8,128)}, bf16[4,4,208,256]{3,2,1...) custom-call(bf16[512,768]{1,0:T(8,128)(2,1)} %bitcast.220, ...), custom_call_target="tpu_custom_call" | custom-call | flops 248000004096 | bytes 31000000 | tf_op jit(solution)/shard_map/middle/pallas_call | solution.py:845
  190.4 9.7 %back_query.2 = (bf16[256,768]{1,0:T(8,128)(2,1)}, f32[256,768]{1,0:T(8,128)}, bf16[2,12,128,128]{3,2,1,0:T(8,128)(2,1)}, f32[1,1]{1,0:T(1,128)}) custom-call(bf16[512,768]{1,0:T(8,128)(2,1)} %get-tuple-element.69.refs_0_, bf16[512,768]{1,0:T(8,128)(2,1)} %get-tuple-element.64.v_ref.refs_1_, bf16[512,3072]{1,0:T(8,128)(2,1)} %get-tuple-element.62.phq_ref.refs_2_, ...), custom_call_target="tpu_custom_call" | custom-call | flops 64000000000 | bytes 8000000 | tf_op jit(solution)/shard_map/back_query/pallas_call | solution.py:894
  202.2 11.6 %grads.1 = (bf16[16,24,3200]{2,1,0:T(8,128)(2,1)}, bf16[16,24,3200]{2,1,0:T(8,128)(2,1)}, bf16[16,120,768]{2,1,0:T(8,128)(2,1)}, bf16[16,120,768]{2,1,0:T(8,128)(2,1)}, f32[1,1]{1,0:T(1,128)}) custom-call(s32[1]{0:T(128)} %bitcast.63.core_ref, bf16[512,768]{1,0:T(8,128)(2,1)} %get-tuple-element.83.attn_ref, bf16[512,768]{1,0:T(8,128)(2,1)} %get-tuple-element.84.dao_ref, ...), custom_call_target="tpu_custom_call" | custom-call | flops 80000000000 | bytes 10000000 | tf_op jit(solution)/shard_map/grads/pallas_call | solution.py:1062
  214.3 20.1 %collective-permute-done.18 = bf16[4,208,256]{2,1,0:T(8,128)(2,1)S(1)} collective-permute-done((bf16[4,208,256]{2,1,0:T(8,128)(2,1)S(1)}, bf16[4,208,256]{2,1,0:T(8,128)(2,1)S(1)}, u32[]{:S(2)}, u32[]{:S(2)}) %collective-permute-start.18) | collective-permute-done | bytes 426016 | tf_op jit(solution)/shard_map/ppermute | solution.py:120
  237.1 9.7 %back_query.3 = (bf16[256,768]{1,0:T(8,128)(2,1)}, f32[256,768]{1,0:T(8,128)}, bf16[2,12,128,128]{3,2,1,0:T(8,128)(2,1)}, f32[1,1]{1,0:T(1,128)}) custom-call(bf16[512,768]{1,0:T(8,128)(2,1)} %get-tuple-element.69.refs_0_, bf16[512,768]{1,0:T(8,128)(2,1)} %get-tuple-element.64.v_ref.refs_1_, bf16[512,3072]{1,0:T(8,128)(2,1)} %get-tuple-element.62.phq_ref.refs_2_, ...), custom_call_target="tpu_custom_call" | custom-call | flops 64000000000 | bytes 8000000 | tf_op jit(solution)/shard_map/back_query/pallas_call | solution.py:894
  246.8 13.6 %collective-permute-done.19 = bf16[4,208,256]{2,1,0:T(8,128)(2,1)S(1)} collective-permute-done((bf16[4,208,256]{2,1,0:T(8,128)(2,1)S(1)}, bf16[4,208,256]{2,1,0:T(8,128)(2,1)S(1)}, u32[]{:S(2)}, u32[]{:S(2)}) %collective-permute-start.19) | collective-permute-done | bytes 426016 | tf_op jit(solution)/shard_map/ppermute | solution.py:120
  262.5 10.4 %collective-permute-done.20 = bf16[4,208,256]{2,1,0:T(8,128)(2,1)S(1)} collective-permute-done((bf16[4,208,256]{2,1,0:T(8,128)(2,1)S(1)}, bf16[4,208,256]{2,1,0:T(8,128)(2,1)S(1)}, u32[]{:S(2)}, u32[]{:S(2)}) %collective-permute-start.20) | collective-permute-done | bytes 426016 | tf_op jit(solution)/shard_map/ppermute | solution.py:120
  287.6 13.5 %back_key.1.dkv_ref = bf16[512,1536]{1,0:T(8,128)(2,1)} custom-call(bf16[512,768]{1,0:T(8,128)(2,1)} %get-tuple-element.75.k_ref, bf16[512,768]{1,0:T(8,128)(2,1)} %get-tuple-element.64.v_ref.refs_1_, bf16[512,3072]{1,0:T(8,128)(2,1)} %get-tuple-element.62.phq_ref.refs_2_, bf16[512,3072]{1,0:T(8,128)(2,1)} %get-tuple-element.63.phk_ref.refs_3_, ...), custom_call_target="tpu_custom_call" | custom-call | flops 103999995904 | bytes 13000000 | tf_op jit(solution)/shard_map/back_key/pallas_call | solution.py:928
  301.1 6.1 %first_grads.1 = (bf16[16,24,1280]{2,1,0:T(8,128)(2,1)}, bf16[16,24,1280]{2,1,0:T(8,128)(2,1)}, bf16[16,24,1152]{2,1,0:T(8,128)(2,1)}, bf16[16,24,1152]{2,1,0:T(8,128)(2,1)}) custom-call(s32[1]{0:T(128)} %bitcast.63.core_ref, bf16[512,768]{1,0:T(8,128)(2,1)} %bitcast.221, bf16[512,768]{1,0:T(8,128)(2,1)} %copy-done.26, bf16[512,1536]{1,0:T(8,128)(2,1)} %back_key.1.dkv_ref), custom_call_target="tpu_custom_call" | custom-call | flops 48000000000 | bytes 6000000 | tf_op jit(solution)/shard_map/first_grads/pallas_call | solution.py:1127
  315.1 4.8 %collective-permute-done.27 = bf16[1,2,2,2,1,120,768]{6,5,4,3,2,1,0:T(8,128)(2,1)} collective-permute-done((bf16[1,2,2,2,1,120,768]{6,5,4,3,2,1,0:T(8,128)(2,1)}, bf16[1,2,2,2,1,120,768]{6,5,4,3,2,1,0:T(8,128)(2,1)}, u32[]{:S(2)}, u32[]{:S(2)}) %collective-permute-start.27) | collective-permute-done | bytes 1474592 | tf_op jit(solution)/shard_map/ppermute | solution.py:19
  326.8 6.2 %collective-permute-done.39 = bf16[1,2,2,1,1,24,3200]{6,5,4,3,2,1,0:T(8,128)(2,1)S(1)} collective-permute-done((bf16[1,2,2,1,1,24,3200]{6,5,4,3,2,1,0:T(8,128)(2,1)S(1)}, bf16[1,2,2,1,1,24,3200]{6,5,4,3,2,1,0:T(8,128)(2,1)S(1)}, u32[]{:S(2)}, u32[]{:S(2)}) %collective-permute-start.39) | collective-permute-done | bytes 614432 | tf_op jit(solution)/shard_map/ppermute | solution.py:19
  333.3 6.6 %input_grad.1 = (bf16[512,768]{1,0:T(8,128)(2,1)}, f32[1,1]{1,0:T(1,128)}) custom-call(bf16[512,768]{1,0:T(8,128)(2,1)} %copy-done.26, bf16[512,1536]{1,0:T(8,128)(2,1)} %back_key.1.dkv_ref, bf16[768,1280]{1,0:T(8,128)(2,1)} %get-tuple-element.60.wa_ref, bf16[768,1152]{1,0:T(8,128)(2,1)} %get-tuple-element.96.wb_ref, f32[512,768]{1,0:T(8,128)} %get-tuple-element.97.dr1_ref, ...), custom_call_target="tpu_custom_call" | custom-call | flops 48000000000 | bytes 6000000 | tf_op jit(solution)/shard_map/input_grad/pallas_call | solution.py:1158
  340.9 7.0 %collective-permute-done.32 = bf16[2,2,2,1,1,24,1152]{6,5,4,3,2,1,0:T(8,128)(2,1)S(1)} collective-permute-done((bf16[2,2,2,1,1,24,1152]{6,5,4,3,2,1,0:T(8,128)(2,1)S(1)}, bf16[2,2,2,1,1,24,1152]{6,5,4,3,2,1,0:T(8,128)(2,1)S(1)}, u32[]{:S(2)}, u32[]{:S(2)}) %collective-permute-start.32) | collective-permute-done | bytes 442400 | tf_op jit(solution)/shard_map/ppermute | solution.py:19
  355.1 5.0 %collective-permute-done.34 = bf16[1,2,1,1,1,24,1152]{6,5,4,3,2,1,0:T(8,128)(2,1)S(1)} collective-permute-done((bf16[1,2,1,1,1,24,1152]{6,5,4,3,2,1,0:T(8,128)(2,1)S(1)}, bf16[1,2,1,1,1,24,1152]{6,5,4,3,2,1,0:T(8,128)(2,1)S(1)}, u32[]{:S(2)}, u32[]{:S(2)}) %collective-permute-start.34) | collective-permute-done | bytes 110624 | tf_op jit(solution)/shard_map/ppermute | solution.py:19
  367.6 4.7 %collective-permute-done.30 = bf16[1,2,1,1,1,24,1280]{6,5,4,3,2,1,0:T(8,128)(2,1)S(1)} collective-permute-done((bf16[1,2,1,1,1,24,1280]{6,5,4,3,2,1,0:T(8,128)(2,1)S(1)}, bf16[1,2,1,1,1,24,1280]{6,5,4,3,2,1,0:T(8,128)(2,1)S(1)}, u32[]{:S(2)}, u32[]{:S(2)}) %collective-permute-start.30) | collective-permute-done | bytes 122912 | tf_op jit(solution)/shard_map/ppermute | solution.py:19
  (279 shorter events, 129.7 us)
Async XLA Ops:
  7.2 142.7 %all-gather.2.cloned.1.call-start = ((), (), s32[]{:S(2)}) async-start(), calls=%async_computation | async-start | bytes 11151360 | tf_op jit(solution)/shard_map/all_gather | solution.py:1235
  9.7 12.3 %collective-permute-start = (bf16[1,24,1280]{2,1,0:T(8,128)(2,1)S(1)}, bf16[1,24,1280]{2,1,0:T(8,128)(2,1)S(1)}, u32[]{:S(2)}, u32[]{:S(2)}) collective-permute-start(bf16[1,24,1280]{2,1,0:T(8,128)(2,1)S(1)} %maximum_bitcast_fusion), channel_id=1, source_target_pairs={{0,8},{1,9},{2,10},{3,11},{4,12},{5,13},{6,14},{7,15},{8,0},{9,1},... | collective-permute-start | bytes 184328 | tf_op jit(solution)/shard_map/ppermute | solution.py:19
  34.5 11.2 %collective-permute-start.3 = (bf16[8,24,1280]{2,1,0:T(8,128)(2,1)S(1)}, bf16[8,24,1280]{2,1,0:T(8,128)(2,1)S(1)}, u32[]{:S(2)}, u32[]{:S(2)}) collective-permute-start(bf16[8,24,1280]{2,1,0:T(8,128)(2,1)S(1)} %pad_maximum_fusion.3), channel_id=1, source_target_pairs={{0,16},{1,17},{2,18},{3,19},{4,20},{5,21},{6,22},{7,23},{8,24},{9,... | collective-permute-start | bytes 1474568 | tf_op jit(solution)/shard_map/ppermute | solution.py:19
  35.9 11.5 %collective-permute-start.8 = (bf16[8,24,1152]{2,1,0:T(8,128)(2,1)S(1)}, bf16[8,24,1152]{2,1,0:T(8,128)(2,1)S(1)}, u32[]{:S(2)}, u32[]{:S(2)}) collective-permute-start(bf16[8,24,1152]{2,1,0:T(8,128)(2,1)S(1)} %pad_maximum_fusion.4), channel_id=1, source_target_pairs={{0,2},{1,3},{2,0},{3,1},{4,6},{5,7},{6,4},{7,5},{8,10},{9,11},{10,... | collective-permute-start | bytes 1327112 | tf_op jit(solution)/shard_map/ppermute | solution.py:19
  73.2 17.9 %collective-permute-start.11 = (bf16[4,208,256]{2,1,0:T(8,128)(2,1)S(1)}, bf16[4,208,256]{2,1,0:T(8,128)(2,1)S(1)}, u32[]{:S(2)}, u32[]{:S(2)}) collective-permute-start(bf16[4,208,256]{2,1,0:T(8,128)(2,1)S(1)} %fusion.20), channel_id=1, source_target_pairs={{0,2},{1,3},{2,0},{3,1},{4,6},{5,7},{6,4},{7,5},{8,10},{9,11},{10,... | collective-permute-start | bytes 1277960 | tf_op jit(solution)/shard_map/ppermute | solution.py:120
  92.0 16.8 %collective-permute-start.12 = (bf16[4,208,256]{2,1,0:T(8,128)(2,1)S(1)}, bf16[4,208,256]{2,1,0:T(8,128)(2,1)S(1)}, u32[]{:S(2)}, u32[]{:S(2)}) collective-permute-start(bf16[4,208,256]{2,1,0:T(8,128)(2,1)S(1)} %fusion.25), channel_id=1, source_target_pairs={{0,4},{1,5},{2,6},{3,7},{4,8},{5,9},{6,10},{7,11},{8,12},{9,13},{1... | collective-permute-start | bytes 1277960 | tf_op jit(solution)/shard_map/ppermute | solution.py:120
  109.7 23.8 %collective-permute-start.13 = (bf16[4,208,256]{2,1,0:T(8,128)(2,1)S(1)}, bf16[4,208,256]{2,1,0:T(8,128)(2,1)S(1)}, u32[]{:S(2)}, u32[]{:S(2)}) collective-permute-start(bf16[4,208,256]{2,1,0:T(8,128)(2,1)S(1)} %fusion.12), channel_id=1, source_target_pairs={{0,8},{1,9},{2,10},{3,11},{4,12},{5,13},{6,14},{7,15},{16,24},{17,... | collective-permute-start | bytes 1277960 | tf_op jit(solution)/shard_map/ppermute | solution.py:120
  134.0 9.9 %collective-permute-start.14 = (bf16[4,208,256]{2,1,0:T(8,128)(2,1)S(1)}, bf16[4,208,256]{2,1,0:T(8,128)(2,1)S(1)}, u32[]{:S(2)}, u32[]{:S(2)}) collective-permute-start(bf16[4,208,256]{2,1,0:T(8,128)(2,1)S(1)} %get-tuple-element.124), channel_id=1, source_target_pairs={{0,2},{1,3},{2,0},{3,1},{4,6},{5,7},{6,4},{7,5},{8,10},{9,11},{10,... | collective-permute-start | bytes 1277960 | tf_op jit(solution)/shard_map/ppermute | solution.py:120
  187.4 13.2 %collective-permute-start.17 = (bf16[4,208,256]{2,1,0:T(8,128)(2,1)S(1)}, bf16[4,208,256]{2,1,0:T(8,128)(2,1)S(1)}, u32[]{:S(2)}, u32[]{:S(2)}) collective-permute-start(bf16[4,208,256]{2,1,0:T(8,128)(2,1)S(1)} %fusion.22.tie_ref), channel_id=1, source_target_pairs={{15,13},{14,12},{13,15},{12,14},{11,9},{10,8},{9,11},{8,10},{7,5},... | collective-permute-start | bytes 1277960 | tf_op jit(solution)/shard_map/ppermute | solution.py:120
  200.9 33.6 %collective-permute-start.18 = (bf16[4,208,256]{2,1,0:T(8,128)(2,1)S(1)}, bf16[4,208,256]{2,1,0:T(8,128)(2,1)S(1)}, u32[]{:S(2)}, u32[]{:S(2)}) collective-permute-start(bf16[4,208,256]{2,1,0:T(8,128)(2,1)S(1)} %fusion.24), channel_id=1, source_target_pairs={{15,11},{14,10},{13,9},{12,8},{11,7},{10,6},{9,5},{8,4},{7,3},{6,2... | collective-permute-start | bytes 1277960 | tf_op jit(solution)/shard_map/ppermute | solution.py:120
  213.8 63.3 %collective-permute-start.22 = (bf16[16,120,768]{2,1,0:T(8,128)(2,1)}, bf16[16,120,768]{2,1,0:T(8,128)(2,1)}, u32[]{:S(2)}, u32[]{:S(2)}) collective-permute-start(bf16[16,120,768]{2,1,0:T(8,128)(2,1)} %get-tuple-element.94), channel_id=1, source_target_pairs={{0,1},{1,0},{2,3},{3,2},{4,5},{5,4},{6,7},{7,6},{8,9},{9,8},{10,11... | collective-permute-start | bytes 8847368 | tf_op jit(solution)/shard_map/ppermute | solution.py:19
  213.8 59.5 %collective-permute-start.21 = (bf16[16,24,3200]{2,1,0:T(8,128)(2,1)}, bf16[16,24,3200]{2,1,0:T(8,128)(2,1)}, u32[]{:S(2)}, u32[]{:S(2)}) collective-permute-start(bf16[16,24,3200]{2,1,0:T(8,128)(2,1)} %get-tuple-element.92), channel_id=1, source_target_pairs={{0,1},{1,0},{2,3},{3,2},{4,5},{5,4},{6,7},{7,6},{8,9},{9,8},{10,11... | collective-permute-start | bytes 7372808 | tf_op jit(solution)/shard_map/ppermute | solution.py:19
  235.5 25.0 %collective-permute-start.19 = (bf16[4,208,256]{2,1,0:T(8,128)(2,1)S(1)}, bf16[4,208,256]{2,1,0:T(8,128)(2,1)S(1)}, u32[]{:S(2)}, u32[]{:S(2)}) collective-permute-start(bf16[4,208,256]{2,1,0:T(8,128)(2,1)S(1)} %fusion.17), channel_id=1, source_target_pairs={{15,7},{14,6},{13,5},{12,4},{11,3},{10,2},{9,1},{8,0},{31,23},{30,... | collective-permute-start | bytes 1277960 | tf_op jit(solution)/shard_map/ppermute | solution.py:120
  261.5 11.3 %collective-permute-start.20 = (bf16[4,208,256]{2,1,0:T(8,128)(2,1)S(1)}, bf16[4,208,256]{2,1,0:T(8,128)(2,1)S(1)}, u32[]{:S(2)}, u32[]{:S(2)}) collective-permute-start(bf16[4,208,256]{2,1,0:T(8,128)(2,1)S(1)} %get-tuple-element.122), channel_id=1, source_target_pairs={{15,13},{14,12},{13,15},{12,14},{11,9},{10,8},{9,11},{8,10},{7,5},... | collective-permute-start | bytes 1277960 | tf_op jit(solution)/shard_map/ppermute | solution.py:120
  282.4 29.6 %collective-permute-start.26 = (bf16[2,2,2,1,1,24,3200]{6,5,4,3,2,1,0:T(8,128)(2,1)}, bf16[2,2,2,1,1,24,3200]{6,5,4,3,2,1,0:T(8,128)(2,1)}, u32[]{:S(2)}, u32[]{:S(2)}) collective-permute-start(bf16[2,2,2,1,1,24,3200]{6,5,4,3,2,1,0:T(8,128)(2,1)} %constant_dynamic-slice_fusion.15), channel_id=1, source_target_pairs={{0,2},{1,3},{2,0},{3,1},{4,6},{5,7},{6,4},{7,5},{8,10},{9,11},{10,... | collective-permute-start | bytes 3686408 | tf_op jit(solution)/shard_map/ppermute | solution.py:19
  284.5 35.5 %collective-permute-start.27 = (bf16[1,2,2,2,1,120,768]{6,5,4,3,2,1,0:T(8,128)(2,1)}, bf16[1,2,2,2,1,120,768]{6,5,4,3,2,1,0:T(8,128)(2,1)}, u32[]{:S(2)}, u32[]{:S(2)}) collective-permute-start(bf16[1,2,2,2,1,120,768]{6,5,4,3,2,1,0:T(8,128)(2,1)} %constant_dynamic-slice_fusion.14), channel_id=1, source_target_pairs={{0,16},{1,17},{2,18},{3,19},{4,20},{5,21},{6,22},{7,23},{8,24},{9,... | collective-permute-start | bytes 4423688 | tf_op jit(solution)/shard_map/ppermute | solution.py:19
  307.2 15.7 %collective-permute-start.25 = (bf16[16,24,1152]{2,1,0:T(8,128)(2,1)}, bf16[16,24,1152]{2,1,0:T(8,128)(2,1)S(1)}, u32[]{:S(2)}, u32[]{:S(2)}) collective-permute-start(bf16[16,24,1152]{2,1,0:T(8,128)(2,1)} %get-tuple-element.101), channel_id=1, source_target_pairs={{0,1},{1,0},{2,3},{3,2},{4,5},{5,4},{6,7},{7,6},{8,9},{9,8},{10,11... | collective-permute-start | bytes 2654216 | tf_op jit(solution)/shard_map/ppermute | solution.py:19
  307.2 17.6 %collective-permute-start.24 = (bf16[16,24,1280]{2,1,0:T(8,128)(2,1)}, bf16[16,24,1280]{2,1,0:T(8,128)(2,1)S(1)}, u32[]{:S(2)}, u32[]{:S(2)}) collective-permute-start(bf16[16,24,1280]{2,1,0:T(8,128)(2,1)} %get-tuple-element.99), channel_id=1, source_target_pairs={{0,1},{1,0},{2,3},{3,2},{4,5},{5,4},{6,7},{7,6},{8,9},{9,8},{10,11... | collective-permute-start | bytes 2949128 | tf_op jit(solution)/shard_map/ppermute | solution.py:19
  313.6 19.4 %collective-permute-start.39 = (bf16[1,2,2,1,1,24,3200]{6,5,4,3,2,1,0:T(8,128)(2,1)S(1)}, bf16[1,2,2,1,1,24,3200]{6,5,4,3,2,1,0:T(8,128)(2,1)S(1)}, u32[]{:S(2)}, u32[]{:S(2)}) collective-permute-start(bf16[1,2,2,1,1,24,3200]{6,5,4,3,2,1,0:T(8,128)(2,1)S(1)} %constant_dynamic-slice_fusion.2), channel_id=1, source_target_pairs={{0,16},{1,17},{2,18},{3,19},{4,20},{5,21},{6,22},{7,23},{8,24},{9,... | collective-permute-start | bytes 1843208 | tf_op jit(solution)/shard_map/ppermute | solution.py:19
  321.7 28.1 %collective-permute-start.36 = (bf16[1,2,2,1,1,120,768]{6,5,4,3,2,1,0:T(8,128)(2,1)S(1)}, bf16[1,2,2,1,1,120,768]{6,5,4,3,2,1,0:T(8,128)(2,1)S(1)}, u32[]{:S(2)}, u32[]{:S(2)}) collective-permute-start(bf16[1,2,2,1,1,120,768]{6,5,4,3,2,1,0:T(8,128)(2,1)S(1)} %constant_dynamic-slice_fusion.5), channel_id=1, source_target_pairs={{0,2},{1,3},{2,0},{3,1},{4,6},{5,7},{6,4},{7,5},{8,10},{9,11},{10,... | collective-permute-start | bytes 2211848 | tf_op jit(solution)/shard_map/ppermute | solution.py:19
  323.7 24.3 %collective-permute-start.32 = (bf16[2,2,2,1,1,24,1152]{6,5,4,3,2,1,0:T(8,128)(2,1)S(1)}, bf16[2,2,2,1,1,24,1152]{6,5,4,3,2,1,0:T(8,128)(2,1)S(1)}, u32[]{:S(2)}, u32[]{:S(2)}) collective-permute-start(bf16[2,2,2,1,1,24,1152]{6,5,4,3,2,1,0:T(8,128)(2,1)S(1)} %constant_dynamic-slice_fusion.9), channel_id=1, source_target_pairs={{0,2},{1,3},{2,0},{3,1},{4,6},{5,7},{6,4},{7,5},{8,10},{9,11},{10,... | collective-permute-start | bytes 1327112 | tf_op jit(solution)/shard_map/ppermute | solution.py:19
  325.2 29.1 %collective-permute-start.28 = (bf16[1,2,2,2,1,24,1280]{6,5,4,3,2,1,0:T(8,128)(2,1)S(1)}, bf16[1,2,2,2,1,24,1280]{6,5,4,3,2,1,0:T(8,128)(2,1)S(1)}, u32[]{:S(2)}, u32[]{:S(2)}) collective-permute-start(bf16[1,2,2,2,1,24,1280]{6,5,4,3,2,1,0:T(8,128)(2,1)S(1)} %constant_dynamic-slice_fusion.13), channel_id=1, source_target_pairs={{0,16},{1,17},{2,18},{3,19},{4,20},{5,21},{6,22},{7,23},{8,24},{9,... | collective-permute-start | bytes 1474568 | tf_op jit(solution)/shard_map/ppermute | solution.py:19
  340.9 9.3 %collective-permute-start.41 = (bf16[1,1,1,1,1,24,3200]{6,5,4,3,2,1,0:T(8,128)(2,1)S(1)}, bf16[1,1,1,1,1,24,3200]{6,5,4,3,2,1,0:T(8,128)(2,1)S(1)}, u32[]{:S(2)}, u32[]{:S(2)}) collective-permute-start(bf16[1,1,1,1,1,24,3200]{6,5,4,3,2,1,0:T(8,128)(2,1)S(1)} %constant_dynamic-slice_fusion), channel_id=1, source_target_pairs={{0,8},{1,9},{2,10},{3,11},{4,12},{5,13},{6,14},{7,15},{8,0},{9,1},... | collective-permute-start | bytes 460808 | tf_op jit(solution)/shard_map/ppermute | solution.py:19
  350.0 17.5 %collective-permute-start.37 = (bf16[1,2,1,1,1,120,768]{6,5,4,3,2,1,0:T(8,128)(2,1)S(1)}, bf16[1,2,1,1,1,120,768]{6,5,4,3,2,1,0:T(8,128)(2,1)S(1)}, u32[]{:S(2)}, u32[]{:S(2)}) collective-permute-start(bf16[1,2,1,1,1,120,768]{6,5,4,3,2,1,0:T(8,128)(2,1)S(1)} %constant_dynamic-slice_fusion.4), channel_id=1, source_target_pairs={{0,4},{1,5},{2,6},{3,7},{4,0},{5,1},{6,2},{7,3},{8,12},{9,13},{10,... | collective-permute-start | bytes 1105928 | tf_op jit(solution)/shard_map/ppermute | solution.py:19
  (55 other events, 541.4 us)
Sparse Core Ops, SparseCore 0:
  50.6 99.0 all-gather.1
